TPU v7x, 256 devices: a whole 4x4x8 slice. The times are simulated.
256 devices in a mesh: lon: 16 (over y_hi, x, core), tm: 16 (over y_lo, z).
Axes of the slice: x: 4, y: 4 (y_hi: 2, y_lo: 2; y = y_hi * 2 + y_lo), z: 8, core: 2. Of those that a mesh axis runs over, the one named last changes fastest.
Arguments:
- frames_in: bfloat16 [64, 32, 64, 1536], P('tm', None, 'lon'), may hold values from -6 to 6
- conv_kernel: float32 [3, 3, 1536], replicated, may hold values from -2 to 2
- w_query: bfloat16 [1536, 768], replicated, may hold values from -0.15625 to 0.15625
- w_key: bfloat16 [1536, 768], replicated, may hold values from -0.15625 to 0.15625
- w_value: bfloat16 [1536, 768], replicated, may hold values from -0.15625 to 0.15625
- w_out: bfloat16 [768, 1536], replicated, may hold values from -0.21875 to 0.21875
- norm_gain: float32 [768], replicated, may hold values from 0.1 to 1.9
- log_gate: float32 [64, 6], P('tm'), may hold values from -2.5 to 0
- cam_valid: int32 [64, 6], P('tm'), may hold values 0 or 1
- live_frames: int32 [16], P('tm'), may hold values from 2 to 4, as said below
Outputs:
- mixed_out: bfloat16 [64, 32, 64, 1536], P('tm', None, 'lon')
Inputs may be any that keep to these rules, and one draw needn't show every extreme that they name: Frames of a slab from live_frames on are padding; in every draw some slab has all 4 frames live.
All inputs are finite; a program needn't handle non-finite values. No bound on the sum of `cam_valid` on one device may be relied on, other than what follows from the above.
Results may differ from a plain program's by a relative error of at most 0.011.
Values may be sent and summed in bfloat16 or wider, within the bound.
A program may use at most 64 MiB of HBM per device.

v0:
```python
import jax
import jax.numpy as jnp
from jax import lax
from jax.sharding import PartitionSpec as P

HEADS = 6
HD = 128
CAMS = 6


def passed_along(block, axis, distance):
    devices = range(lax.axis_size(axis))
    route = [(i - distance, i) for i in devices if i - distance in devices]
    return lax.ppermute(block, axis, route)


def extended_2(block, sides, width):
    for axis, dim in sides:
        count = lax.axis_size(axis)
        forward = [(i, i + 1) for i in range(count - 1)]
        forward.append((count - 1, 0))
        backward = [(target, source) for source, target in forward]
        low = lax.ppermute(
            lax.slice_in_dim(block, block.shape[dim] - width, None, axis=dim), axis, forward
        )
        high = lax.ppermute(lax.slice_in_dim(block, 0, width, axis=dim), axis, backward)
        block = jnp.concatenate([low, block, high], axis=dim)
    return block


def slab_chain(whole_decay, slab_final):

    def relay_step(turn_index, incoming):
        outgoing = whole_decay[:, None] * incoming + slab_final
        return passed_along(outgoing, "tm", 1)

    return lax.fori_loop(0, lax.axis_size("tm") - 1, relay_step, jnp.zeros_like(slab_final))


def advance(state_terms, frame_rates, row_owner):
    onehot = (row_owner[None, :] == jnp.arange(HEADS)[:, None]).astype(jnp.float32)
    row_rates = jnp.dot(frame_rates, onehot, precision=lax.Precision.HIGHEST)
    decay = jnp.exp(row_rates)

    def recur(carried, inputs):
        factor, frame_term = inputs
        carried = factor[:, None] * carried + frame_term
        return (carried, carried)

    slab_final, local_states = lax.scan(
        recur, jnp.zeros(state_terms.shape[1:], jnp.float32), (decay, state_terms)
    )
    decay_reach = jnp.exp(jnp.cumsum(row_rates, axis=0))
    incoming = slab_chain(decay_reach[-1], slab_final)
    return local_states + decay_reach[:, :, None] * incoming[None]


def local(
    frames_in,
    conv_kernel,
    w_query,
    w_key,
    w_value,
    w_out,
    norm_gain,
    log_gate,
    cam_valid,
    live_frames,
):
    frame_count, lat_rows, lon_cols, model_width = frames_in.shape
    lon_size = lax.axis_size("lon")
    lon_index = lax.axis_index("lon")
    extended = extended_2(frames_in, (("lon", 2),), 1)
    padded = jnp.pad(extended, ((0, 0), (1, 1), (0, 0), (0, 0)))
    filtered = jnp.zeros((frame_count, lat_rows, lon_cols, model_width), jnp.float32)
    for lat_tap in range(3):
        for lon_tap in range(3):
            window = padded[:, lat_tap : lat_tap + lat_rows, lon_tap : lon_tap + lon_cols].astype(
                jnp.float32
            )
            filtered = filtered + conv_kernel[lat_tap, lon_tap] * window
    mixed = jax.nn.silu(filtered).astype(jnp.bfloat16).reshape(-1, model_width)
    keys = jnp.dot(mixed, w_key, preferred_element_type=jnp.float32).astype(jnp.bfloat16)
    values = jnp.dot(mixed, w_value, preferred_element_type=jnp.float32).astype(jnp.bfloat16)
    queries = jnp.dot(mixed, w_query, preferred_element_type=jnp.float32).astype(jnp.bfloat16)
    columns = lon_index * lon_cols + jnp.arange(lon_cols)
    camera = columns * CAMS // (lon_cols * lon_size)
    onehot = (camera[None, :] == jnp.arange(CAMS)[:, None]).astype(jnp.float32)
    visible = jnp.dot(cam_valid.astype(jnp.float32), onehot, precision=lax.Precision.HIGHEST)
    frame_live = (jnp.arange(frame_count) < live_frames[0]).astype(jnp.float32)
    key_keep = (visible * frame_live[:, None]).astype(jnp.bfloat16)
    kept_keys = (
        keys.reshape(frame_count, lat_rows, lon_cols, HEADS, HD) * key_keep[:, None, :, None, None]
    )
    state_terms = jnp.einsum(
        "fnhd,fnhe->fhde",
        kept_keys.reshape(frame_count, -1, HEADS, HD),
        values.reshape(frame_count, -1, HEADS, HD),
        preferred_element_type=jnp.float32,
    )
    state_terms = state_terms.reshape(frame_count, HEADS * HD, HD)
    frame_rates = log_gate * frame_live[:, None]
    summed = lax.psum(state_terms, "lon")
    row_owner = jnp.arange(HEADS * HD) // HD
    state_rounded = advance(summed, frame_rates, row_owner).astype(jnp.bfloat16)
    query_heads = queries.reshape(frame_count, -1, HEADS, HD)
    state_heads = state_rounded.reshape(frame_count, HEADS, HD, HD)
    readout = jnp.einsum(
        "fnhd,fhde->fnhe", query_heads, state_heads, preferred_element_type=jnp.float32
    )
    inverse_rms = lax.rsqrt(jnp.mean(readout * readout, axis=-1, keepdims=True) + 1e-05)
    normed = (
        (readout * inverse_rms * norm_gain.reshape(HEADS, HD))
        .astype(jnp.bfloat16)
        .reshape(-1, HEADS * HD)
    )
    result = jnp.dot(normed, w_out, preferred_element_type=jnp.float32)
    result = (
        result.reshape(frame_count, lat_rows, lon_cols, model_width)
        * frame_live[:, None, None, None]
    )
    return result.astype(jnp.bfloat16)


def solution(mesh):
    in_specs = (
        P("tm", None, "lon", None),
        P(),
        P(),
        P(),
        P(),
        P(),
        P(),
        P("tm", None),
        P("tm", None),
        P("tm"),
    )
    out_specs = P("tm", None, "lon", None)
    return jax.shard_map(local, mesh=mesh, in_specs=in_specs, out_specs=out_specs, check_vma=False)
```

profile of v0, /device:TPU:8, one launch (start us, length us, event | category | flops | bytes accessed | tf_op | source)
XLA Modules:
  0.0 439.0 jit_solution(2155943032186413763)
XLA Ops:
  6.5 3.4 fusion.31
  10.2 5.4 %collective-permute-start.2 = (bf16[4,32,1,1536]{3,1,2,0:T(8,128)(2,1)S(1)}, bf16[4,32,1,1536]{3,1,2,0:T(8,128)(2,1)}, u32[]{:S(2)}, u32[]{:S(2)}) collective-permute-start(bf16[4,32,1,1536]{3,1,2,0:T(8,128)(2,1)S(1)} %copy.53), channel_id=1, source_target_pairs={{16,0},{32,16},{48,32},{64,48},{80,64},{96,80},{112,96},{128,112},... | collective-permute-start | bytes 1179656 | tf_op jit(solution)/shard_map/ppermute | solution.py:26
  23.2 2.8 fusion.5
  26.0 10.6 %fusion.6 = bf16[4,32,4,1536]{3,2,1,0:T(4,128)(2,1)} fusion(bf16[4,32,4,1536]{3,2,1,0:T(4,128)(2,1)S(1)} %copy-done.1, bf16[4,34,6,1536]{3,2,1,0:T(8,128)(2,1)S(1)} %fusion.5, bf16[4,32,1,1536]{3,2,1,0:T(2,128)(2,1)S(1)} %copy.32, bf16[4,32,1,1536]{3,2,1,0:T(2,128)(2,1)S(1)} %copy.31, f32[1536]{0:T(1024)S(1)} %get-tuple-element.83, ...), kind=kLoop, calls=%fused_computation.15 | loop fusion | flops 29097984 | bytes 13424640 | tf_op jit(solution)/shard_map/convert_element_type | solution.py:82
  36.6 3.7 reshape.94
  40.3 4.4 %convolution_convert_fusion.2 = bf16[512,768]{1,0:T(8,128)(2,1)} fusion(bf16[512,1536]{1,0:T(8,128)(2,1)} %reshape.94, bf16[1536,768]{1,0:T(8,128)(2,1)} %param.17), kind=kOutput, calls=%fused_computation.28 | convolution fusion | flops 1208352768 | bytes 4718592 | tf_op jit(solution)/shard_map/dot_general | solution.py:83
  47.2 4.4 %convolution_convert_fusion.1 = bf16[512,768]{1,0:T(8,128)(2,1)} fusion(bf16[512,1536]{1,0:T(8,128)(2,1)} %reshape.94, bf16[1536,768]{1,0:T(8,128)(2,1)} %param.18), kind=kOutput, calls=%fused_computation.27 | convolution fusion | flops 1208352768 | bytes 4718592 | tf_op jit(solution)/shard_map/dot_general | solution.py:84
  51.6 2.0 reshape.101
  57.8 3.5 convolution_convert_fusion
  63.2 142.9 %all-reduce.3.cloned.1.call-done = f32[4,768,128]{2,1,0:T(8,128)} async-done(((f32[4,768,128]{2,1,0:T(8,128)}), f32[4,768,128]{2,1,0:T(8,128)}) %all-reduce.3.cloned.1.call-update) | async-done | bytes 1572880 | tf_op jit(solution)/shard_map/psum | solution.py:103
  206.2 10.9 %while.24 = (s32[]{:T(128)}, f32[768,128]{1,0:T(8,128)S(1)}, f32[4,768,128]{2,1,0:T(8,128)}, f32[4,768]{1,0:T(4,128)}, f32[4,768,128]{2,1,0:T(8,128)}, /*index=5*/s32[]{:T(128)}, s32[]{:T(128)}) while((s32[]{:T(128)}, f32[768,128]{1,0:T(8,128)S(1)}, f32[4,768,128]{2,1,0:T(8,128)}, f32[4,768]{1,0:T(4,128)}, ...), condition=%wide.region_2.3_spmd.clone, body=%wide.region_1.2_spmd.clone.sunk | while | flops 294915 | bytes 1582683 | solution.py:50
  206.9 2.0 bitcast_dynamic-update-slice_fusion.2
  209.6 2.0 bitcast_dynamic-update-slice_fusion.2
  212.3 2.0 bitcast_dynamic-update-slice_fusion.2
  215.1 2.0 bitcast_dynamic-update-slice_fusion.2
  217.1 203.1 %while.23 = (s32[]{:T(128)}, f32[768,128]{1,0:T(8,128)S(1)}, f32[1,768]{1,0:T(1,128)S(1)}, f32[768,128]{1,0:T(8,128)S(1)}, s32[]{:T(128)}, /*index=5*/f32[]{:T(128)}) while((s32[]{:T(128)}, f32[768,128]{1,0:T(8,128)S(1)}, f32[1,768]{1,0:T(1,128)S(1)}, f32[768,128]{1,0:T(8,128)S(1)}, s32[]{:T(128)}, /*index=5*/f32[]{:T(128)}) %tuple.52), condition=%wide.region_5.6_spmd, body=%wide.region_4.5_spmd.sunk | while | flops 196610 | bytes 2761841 | solution.py:37
  217.3 3.5 collective-permute-start
  220.8 11.1 %collective-permute-done = f32[768,128]{1,0:T(8,128)S(1)} collective-permute-done((f32[768,128]{1,0:T(8,128)S(1)}, f32[768,128]{1,0:T(8,128)S(1)}, u32[]{:S(2)}, u32[]{:S(2)}) %collective-permute-start) | collective-permute-done | bytes 393248 | tf_op jit(solution)/shard_map/while/body/eval_jaxpr/ppermute | solution.py:14
  232.1 1.9 collective-permute-start
  234.0 11.8 %collective-permute-done = f32[768,128]{1,0:T(8,128)S(1)} collective-permute-done((f32[768,128]{1,0:T(8,128)S(1)}, f32[768,128]{1,0:T(8,128)S(1)}, u32[]{:S(2)}, u32[]{:S(2)}) %collective-permute-start) | collective-permute-done | bytes 393248 | tf_op jit(solution)/shard_map/while/body/eval_jaxpr/ppermute | solution.py:14
  245.9 1.9 collective-permute-start
  247.9 10.8 %collective-permute-done = f32[768,128]{1,0:T(8,128)S(1)} collective-permute-done((f32[768,128]{1,0:T(8,128)S(1)}, f32[768,128]{1,0:T(8,128)S(1)}, u32[]{:S(2)}, u32[]{:S(2)}) %collective-permute-start) | collective-permute-done | bytes 393248 | tf_op jit(solution)/shard_map/while/body/eval_jaxpr/ppermute | solution.py:14
  258.9 1.9 collective-permute-start
  260.8 9.9 %collective-permute-done = f32[768,128]{1,0:T(8,128)S(1)} collective-permute-done((f32[768,128]{1,0:T(8,128)S(1)}, f32[768,128]{1,0:T(8,128)S(1)}, u32[]{:S(2)}, u32[]{:S(2)}) %collective-permute-start) | collective-permute-done | bytes 393248 | tf_op jit(solution)/shard_map/while/body/eval_jaxpr/ppermute | solution.py:14
  270.9 1.9 collective-permute-start
  272.9 9.8 %collective-permute-done = f32[768,128]{1,0:T(8,128)S(1)} collective-permute-done((f32[768,128]{1,0:T(8,128)S(1)}, f32[768,128]{1,0:T(8,128)S(1)}, u32[]{:S(2)}, u32[]{:S(2)}) %collective-permute-start) | collective-permute-done | bytes 393248 | tf_op jit(solution)/shard_map/while/body/eval_jaxpr/ppermute | solution.py:14
  282.9 1.9 collective-permute-start
  284.8 9.8 %collective-permute-done = f32[768,128]{1,0:T(8,128)S(1)} collective-permute-done((f32[768,128]{1,0:T(8,128)S(1)}, f32[768,128]{1,0:T(8,128)S(1)}, u32[]{:S(2)}, u32[]{:S(2)}) %collective-permute-start) | collective-permute-done | bytes 393248 | tf_op jit(solution)/shard_map/while/body/eval_jaxpr/ppermute | solution.py:14
  294.9 1.9 collective-permute-start
  296.8 10.8 %collective-permute-done = f32[768,128]{1,0:T(8,128)S(1)} collective-permute-done((f32[768,128]{1,0:T(8,128)S(1)}, f32[768,128]{1,0:T(8,128)S(1)}, u32[]{:S(2)}, u32[]{:S(2)}) %collective-permute-start) | collective-permute-done | bytes 393248 | tf_op jit(solution)/shard_map/while/body/eval_jaxpr/ppermute | solution.py:14
  307.8 1.9 collective-permute-start
  309.8 11.9 %collective-permute-done = f32[768,128]{1,0:T(8,128)S(1)} collective-permute-done((f32[768,128]{1,0:T(8,128)S(1)}, f32[768,128]{1,0:T(8,128)S(1)}, u32[]{:S(2)}, u32[]{:S(2)}) %collective-permute-start) | collective-permute-done | bytes 393248 | tf_op jit(solution)/shard_map/while/body/eval_jaxpr/ppermute | solution.py:14
  321.9 1.9 collective-permute-start
  323.8 13.1 %collective-permute-done = f32[768,128]{1,0:T(8,128)S(1)} collective-permute-done((f32[768,128]{1,0:T(8,128)S(1)}, f32[768,128]{1,0:T(8,128)S(1)}, u32[]{:S(2)}, u32[]{:S(2)}) %collective-permute-start) | collective-permute-done | bytes 393248 | tf_op jit(solution)/shard_map/while/body/eval_jaxpr/ppermute | solution.py:14
  337.1 1.9 collective-permute-start
  339.0 13.9 %collective-permute-done = f32[768,128]{1,0:T(8,128)S(1)} collective-permute-done((f32[768,128]{1,0:T(8,128)S(1)}, f32[768,128]{1,0:T(8,128)S(1)}, u32[]{:S(2)}, u32[]{:S(2)}) %collective-permute-start) | collective-permute-done | bytes 393248 | tf_op jit(solution)/shard_map/while/body/eval_jaxpr/ppermute | solution.py:14
  353.1 1.9 collective-permute-start
  355.0 13.0 %collective-permute-done = f32[768,128]{1,0:T(8,128)S(1)} collective-permute-done((f32[768,128]{1,0:T(8,128)S(1)}, f32[768,128]{1,0:T(8,128)S(1)}, u32[]{:S(2)}, u32[]{:S(2)}) %collective-permute-start) | collective-permute-done | bytes 393248 | tf_op jit(solution)/shard_map/while/body/eval_jaxpr/ppermute | solution.py:14
  368.3 1.9 collective-permute-start
  370.2 12.2 %collective-permute-done = f32[768,128]{1,0:T(8,128)S(1)} collective-permute-done((f32[768,128]{1,0:T(8,128)S(1)}, f32[768,128]{1,0:T(8,128)S(1)}, u32[]{:S(2)}, u32[]{:S(2)}) %collective-permute-start) | collective-permute-done | bytes 393248 | tf_op jit(solution)/shard_map/while/body/eval_jaxpr/ppermute | solution.py:14
  382.6 1.9 collective-permute-start
  384.5 11.3 %collective-permute-done = f32[768,128]{1,0:T(8,128)S(1)} collective-permute-done((f32[768,128]{1,0:T(8,128)S(1)}, f32[768,128]{1,0:T(8,128)S(1)}, u32[]{:S(2)}, u32[]{:S(2)}) %collective-permute-start) | collective-permute-done | bytes 393248 | tf_op jit(solution)/shard_map/while/body/eval_jaxpr/ppermute | solution.py:14
  396.0 1.9 collective-permute-start
  397.9 10.3 %collective-permute-done = f32[768,128]{1,0:T(8,128)S(1)} collective-permute-done((f32[768,128]{1,0:T(8,128)S(1)}, f32[768,128]{1,0:T(8,128)S(1)}, u32[]{:S(2)}, u32[]{:S(2)}) %collective-permute-start) | collective-permute-done | bytes 393248 | tf_op jit(solution)/shard_map/while/body/eval_jaxpr/ppermute | solution.py:14
  410.4 9.8 %collective-permute-done = f32[768,128]{1,0:T(8,128)S(1)} collective-permute-done((f32[768,128]{1,0:T(8,128)S(1)}, f32[768,128]{1,0:T(8,128)S(1)}, u32[]{:S(2)}, u32[]{:S(2)}) %collective-permute-start) | collective-permute-done | bytes 393248 | tf_op jit(solution)/shard_map/while/body/eval_jaxpr/ppermute | solution.py:14
  420.2 2.0 add_convert_fusion
  427.3 2.5 fusion.7
  429.8 2.4 copy.45
  (84 shorter events, 28.2 us)
Async XLA Ops:
  6.5 420.7 %copy-start = (bf16[768,1536]{1,0:T(8,128)(2,1)S(1)}, bf16[768,1536]{1,0:T(8,128)(2,1)}, u32[]{:S(2)}) copy-start(bf16[768,1536]{1,0:T(8,128)(2,1)} %param.19) | copy-start | bytes 7077892
  6.5 9.7 %copy-start.5 = (s32[4,6]{1,0:T(4,128)S(1)}, s32[4,6]{1,0:T(4,128)}, u32[]{:S(2)}) copy-start(s32[4,6]{1,0:T(4,128)} %param.22) | copy-start | bytes 292
  6.5 199.6 %all-reduce.3.cloned.1.call-start = ((), (), s32[]{:S(2)}) async-start(), calls=%async_computation | async-start | bytes 3145728 | tf_op jit(solution)/shard_map/psum | solution.py:103
  10.0 10.9 %collective-permute-start.1 = (bf16[4,32,1,1536]{3,1,2,0:T(8,128)(2,1)S(1)}, bf16[4,32,1,1536]{3,1,2,0:T(8,128)(2,1)S(1)}, u32[]{:S(2)}, u32[]{:S(2)}) collective-permute-start(bf16[4,32,1,1536]{3,1,2,0:T(8,128)(2,1)S(1)} %copy.52), channel_id=1, source_target_pairs={{0,16},{16,32},{32,48},{48,64},{64,80},{80,96},{96,112},{112,128},... | collective-permute-start | bytes 1179656 | tf_op jit(solution)/shard_map/ppermute | solution.py:23
  10.2 11.4 %collective-permute-start.2 = (bf16[4,32,1,1536]{3,1,2,0:T(8,128)(2,1)S(1)}, bf16[4,32,1,1536]{3,1,2,0:T(8,128)(2,1)}, u32[]{:S(2)}, u32[]{:S(2)}) collective-permute-start(bf16[4,32,1,1536]{3,1,2,0:T(8,128)(2,1)S(1)} %copy.53), channel_id=1, source_target_pairs={{16,0},{32,16},{48,32},{64,48},{80,64},{96,80},{112,96},{128,112},... | collective-permute-start | bytes 1179656 | tf_op jit(solution)/shard_map/ppermute | solution.py:26
  18.1 5.1 %copy-start.1 = (bf16[4,32,4,1536]{3,2,1,0:T(4,128)(2,1)S(1)}, bf16[4,32,4,1536]{3,2,1,0:T(4,128)(2,1)}, u32[]{:S(2)}) copy-start(bf16[4,32,4,1536]{3,2,1,0:T(4,128)(2,1)} %param.14) | copy-start | bytes 4718596
  54.8 1.6 copy-start.6
  57.2 0.6 copy-start.3
  217.3 14.6 %collective-permute-start = (f32[768,128]{1,0:T(8,128)S(1)}, f32[768,128]{1,0:T(8,128)S(1)}, u32[]{:S(2)}, u32[]{:S(2)}) collective-permute-start(f32[768,128]{1,0:T(8,128)S(1)} %multiply_add_fusion.2), channel_id=1, source_target_pairs={{0,1},{1,2},{2,3},{3,4},{4,5},{5,6},{6,7},{7,8},{8,9},{9,10},{10,1... | collective-permute-start | bytes 1179656 | tf_op jit(solution)/shard_map/while/body/eval_jaxpr/ppermute | solution.py:14
  232.1 13.7 %collective-permute-start = (f32[768,128]{1,0:T(8,128)S(1)}, f32[768,128]{1,0:T(8,128)S(1)}, u32[]{:S(2)}, u32[]{:S(2)}) collective-permute-start(f32[768,128]{1,0:T(8,128)S(1)} %multiply_add_fusion.2), channel_id=1, source_target_pairs={{0,1},{1,2},{2,3},{3,4},{4,5},{5,6},{6,7},{7,8},{8,9},{9,10},{10,1... | collective-permute-start | bytes 1179656 | tf_op jit(solution)/shard_map/while/body/eval_jaxpr/ppermute | solution.py:14
  245.9 12.8 %collective-permute-start = (f32[768,128]{1,0:T(8,128)S(1)}, f32[768,128]{1,0:T(8,128)S(1)}, u32[]{:S(2)}, u32[]{:S(2)}) collective-permute-start(f32[768,128]{1,0:T(8,128)S(1)} %multiply_add_fusion.2), channel_id=1, source_target_pairs={{0,1},{1,2},{2,3},{3,4},{4,5},{5,6},{6,7},{7,8},{8,9},{9,10},{10,1... | collective-permute-start | bytes 1179656 | tf_op jit(solution)/shard_map/while/body/eval_jaxpr/ppermute | solution.py:14
  258.9 11.8 %collective-permute-start = (f32[768,128]{1,0:T(8,128)S(1)}, f32[768,128]{1,0:T(8,128)S(1)}, u32[]{:S(2)}, u32[]{:S(2)}) collective-permute-start(f32[768,128]{1,0:T(8,128)S(1)} %multiply_add_fusion.2), channel_id=1, source_target_pairs={{0,1},{1,2},{2,3},{3,4},{4,5},{5,6},{6,7},{7,8},{8,9},{9,10},{10,1... | collective-permute-start | bytes 1179656 | tf_op jit(solution)/shard_map/while/body/eval_jaxpr/ppermute | solution.py:14
  270.9 11.8 %collective-permute-start = (f32[768,128]{1,0:T(8,128)S(1)}, f32[768,128]{1,0:T(8,128)S(1)}, u32[]{:S(2)}, u32[]{:S(2)}) collective-permute-start(f32[768,128]{1,0:T(8,128)S(1)} %multiply_add_fusion.2), channel_id=1, source_target_pairs={{0,1},{1,2},{2,3},{3,4},{4,5},{5,6},{6,7},{7,8},{8,9},{9,10},{10,1... | collective-permute-start | bytes 1179656 | tf_op jit(solution)/shard_map/while/body/eval_jaxpr/ppermute | solution.py:14
  282.9 11.8 %collective-permute-start = (f32[768,128]{1,0:T(8,128)S(1)}, f32[768,128]{1,0:T(8,128)S(1)}, u32[]{:S(2)}, u32[]{:S(2)}) collective-permute-start(f32[768,128]{1,0:T(8,128)S(1)} %multiply_add_fusion.2), channel_id=1, source_target_pairs={{0,1},{1,2},{2,3},{3,4},{4,5},{5,6},{6,7},{7,8},{8,9},{9,10},{10,1... | collective-permute-start | bytes 1179656 | tf_op jit(solution)/shard_map/while/body/eval_jaxpr/ppermute | solution.py:14
  294.9 12.8 %collective-permute-start = (f32[768,128]{1,0:T(8,128)S(1)}, f32[768,128]{1,0:T(8,128)S(1)}, u32[]{:S(2)}, u32[]{:S(2)}) collective-permute-start(f32[768,128]{1,0:T(8,128)S(1)} %multiply_add_fusion.2), channel_id=1, source_target_pairs={{0,1},{1,2},{2,3},{3,4},{4,5},{5,6},{6,7},{7,8},{8,9},{9,10},{10,1... | collective-permute-start | bytes 1179656 | tf_op jit(solution)/shard_map/while/body/eval_jaxpr/ppermute | solution.py:14
  307.8 13.8 %collective-permute-start = (f32[768,128]{1,0:T(8,128)S(1)}, f32[768,128]{1,0:T(8,128)S(1)}, u32[]{:S(2)}, u32[]{:S(2)}) collective-permute-start(f32[768,128]{1,0:T(8,128)S(1)} %multiply_add_fusion.2), channel_id=1, source_target_pairs={{0,1},{1,2},{2,3},{3,4},{4,5},{5,6},{6,7},{7,8},{8,9},{9,10},{10,1... | collective-permute-start | bytes 1179656 | tf_op jit(solution)/shard_map/while/body/eval_jaxpr/ppermute | solution.py:14
  321.9 15.0 %collective-permute-start = (f32[768,128]{1,0:T(8,128)S(1)}, f32[768,128]{1,0:T(8,128)S(1)}, u32[]{:S(2)}, u32[]{:S(2)}) collective-permute-start(f32[768,128]{1,0:T(8,128)S(1)} %multiply_add_fusion.2), channel_id=1, source_target_pairs={{0,1},{1,2},{2,3},{3,4},{4,5},{5,6},{6,7},{7,8},{8,9},{9,10},{10,1... | collective-permute-start | bytes 1179656 | tf_op jit(solution)/shard_map/while/body/eval_jaxpr/ppermute | solution.py:14
  337.1 15.8 %collective-permute-start = (f32[768,128]{1,0:T(8,128)S(1)}, f32[768,128]{1,0:T(8,128)S(1)}, u32[]{:S(2)}, u32[]{:S(2)}) collective-permute-start(f32[768,128]{1,0:T(8,128)S(1)} %multiply_add_fusion.2), channel_id=1, source_target_pairs={{0,1},{1,2},{2,3},{3,4},{4,5},{5,6},{6,7},{7,8},{8,9},{9,10},{10,1... | collective-permute-start | bytes 1179656 | tf_op jit(solution)/shard_map/while/body/eval_jaxpr/ppermute | solution.py:14
  353.1 15.0 %collective-permute-start = (f32[768,128]{1,0:T(8,128)S(1)}, f32[768,128]{1,0:T(8,128)S(1)}, u32[]{:S(2)}, u32[]{:S(2)}) collective-permute-start(f32[768,128]{1,0:T(8,128)S(1)} %multiply_add_fusion.2), channel_id=1, source_target_pairs={{0,1},{1,2},{2,3},{3,4},{4,5},{5,6},{6,7},{7,8},{8,9},{9,10},{10,1... | collective-permute-start | bytes 1179656 | tf_op jit(solution)/shard_map/while/body/eval_jaxpr/ppermute | solution.py:14
  368.3 14.1 %collective-permute-start = (f32[768,128]{1,0:T(8,128)S(1)}, f32[768,128]{1,0:T(8,128)S(1)}, u32[]{:S(2)}, u32[]{:S(2)}) collective-permute-start(f32[768,128]{1,0:T(8,128)S(1)} %multiply_add_fusion.2), channel_id=1, source_target_pairs={{0,1},{1,2},{2,3},{3,4},{4,5},{5,6},{6,7},{7,8},{8,9},{9,10},{10,1... | collective-permute-start | bytes 1179656 | tf_op jit(solution)/shard_map/while/body/eval_jaxpr/ppermute | solution.py:14
  382.6 13.2 %collective-permute-start = (f32[768,128]{1,0:T(8,128)S(1)}, f32[768,128]{1,0:T(8,128)S(1)}, u32[]{:S(2)}, u32[]{:S(2)}) collective-permute-start(f32[768,128]{1,0:T(8,128)S(1)} %multiply_add_fusion.2), channel_id=1, source_target_pairs={{0,1},{1,2},{2,3},{3,4},{4,5},{5,6},{6,7},{7,8},{8,9},{9,10},{10,1... | collective-permute-start | bytes 1179656 | tf_op jit(solution)/shard_map/while/body/eval_jaxpr/ppermute | solution.py:14
  396.0 12.3 %collective-permute-start = (f32[768,128]{1,0:T(8,128)S(1)}, f32[768,128]{1,0:T(8,128)S(1)}, u32[]{:S(2)}, u32[]{:S(2)}) collective-permute-start(f32[768,128]{1,0:T(8,128)S(1)} %multiply_add_fusion.2), channel_id=1, source_target_pairs={{0,1},{1,2},{2,3},{3,4},{4,5},{5,6},{6,7},{7,8},{8,9},{9,10},{10,1... | collective-permute-start | bytes 1179656 | tf_op jit(solution)/shard_map/while/body/eval_jaxpr/ppermute | solution.py:14
  408.4 11.8 %collective-permute-start = (f32[768,128]{1,0:T(8,128)S(1)}, f32[768,128]{1,0:T(8,128)S(1)}, u32[]{:S(2)}, u32[]{:S(2)}) collective-permute-start(f32[768,128]{1,0:T(8,128)S(1)} %multiply_add_fusion.2), channel_id=1, source_target_pairs={{0,1},{1,2},{2,3},{3,4},{4,5},{5,6},{6,7},{7,8},{8,9},{9,10},{10,1... | collective-permute-start | bytes 1179656 | tf_op jit(solution)/shard_map/while/body/eval_jaxpr/ppermute | solution.py:14
  420.2 2.0 copy-start.2
  420.2 2.7 copy-start.4
Sparse Core Ops, SparseCore 0:
  56.5 149.6 all-reduce.2
where the time goes:
time: 440 us; the launch traced here: 439 us
  waiting for transfers between devices  314 us (71%)
  starting transfers between devices  35.9 us (8%)
  other arithmetic  28.5 us (6%)
  local copies, waits for them, and re-layouts  27.6 us (6%)
  matrix products  18.1 us (4%)
  between operations  14.3 us (3%)
    ppermute x15, waiting for transfers between devices, passed_along(): return lax.ppermute(block, axis, route)  170 us
    psum x1, waiting for transfers between devices, local(): summed = lax.psum(state_terms, 'lon')  143 us
    ppermute x15, starting transfers between devices, passed_along(): return lax.ppermute(block, axis, route)  30.4 us
    convert_element_type x1, other arithmetic, local(): mixed = jax.nn.silu(filtered).astype(jnp.bfloat16).reshape(-1, model_width)  10.6 us
  transfers between devices with their start and end apart: 18, of which 17 were waited for; matrix products, arithmetic and copies ran while one was open for 2% of the time, Pallas kernels for 0%

commit v1 on v0

v1 whole, which is shorter than its diff:
```python
import functools

import jax
import jax.numpy as jnp
from jax import lax
from jax.experimental import pallas as pl
from jax.experimental.pallas import tpu as pltpu
from jax.sharding import PartitionSpec as P

MESH = pl.DeviceIdType.MESH
F32 = jnp.float32
BF16 = jnp.bfloat16

HEADS = 6
HD = 128
CAMS = 6
FRAMES = 4
LAT = 32
COLS = 4
D = 1536
HK = HEADS * HD
TOK = LAT * COLS
LONG = 64
CHUNK = 256
HALF = FRAMES * 2 * LAT
OWN = HK // 2
CHIPS = 8
PIECE = OWN // CHIPS
SLABS = 16
LONS = 16


def repeat(first, last, body):
    def step(i, carry):
        body(i)
        return carry

    lax.fori_loop(first, last, step, 0)


def dot(a, b):
    return jnp.dot(a, b, preferred_element_type=F32)


def column_of(t):
    block = t // LAT
    return jnp.where(block == 0, 1, jnp.where(block == 1, 2, jnp.where(block == 2, 0, 3)))


def kernel(
    x_hbm,
    ck_hbm,
    wq_hbm,
    wk_hbm,
    wv_hbm,
    wo_hbm,
    gain_hbm,
    lg_hbm,
    cam_hbm,
    live_ref,
    out_hbm,
    x_v,
    ck,
    wq,
    wk,
    wv,
    wo,
    gain,
    lg,
    cam,
    shift3,
    shift_h,
    order,
    edge_out,
    edge_in,
    partial,
    mixed,
    q_v,
    k_v,
    v_v,
    keep,
    dec,
    reach,
    other,
    own,
    abuf,
    bsend,
    bbuf,
    tmsg,
    tbuf,
    tdec,
    states,
    inc,
    normed,
    out_v,
    load_sem,
    out_sem,
    halo_send,
    halo_recv,
    a_send,
    a_recv,
    b_send,
    b_recv,
    t_send,
    t_recv,
    c_send,
    c_recv,
    d_send,
    d_recv,
    i_send,
    i_recv,
):
    lon = lax.axis_index("lon")
    slab = lax.axis_index("tm")
    core = lon % 2
    chip = lon // 2
    partner = lon + 1 - 2 * core
    mine = pl.multiple_of(core * OWN + chip * PIECE, 16)
    mine_own = pl.multiple_of(chip * PIECE, 16)

    loads = []
    for n, (src, dst) in enumerate(
        (
            (x_hbm, x_v),
            (ck_hbm, ck),
            (lg_hbm, lg),
            (cam_hbm, cam),
            (gain_hbm, gain),
            (wk_hbm, wk),
            (wv_hbm, wv),
            (wq_hbm, wq),
            (wo_hbm, wo),
        )
    ):
        copy = pltpu.make_async_copy(src, dst, load_sem.at[n])
        copy.start()
        loads.append(copy)
    l_x, l_ck, l_lg, l_cam, l_gain, l_wk, l_wv, l_wq, l_wo = loads

    barrier = pltpu.get_barrier_semaphore()

    def greet(d):
        pl.semaphore_signal(
            barrier, inc=1, device_id={"lon": (lon + d) % LONS}, device_id_type=MESH
        )
        pl.semaphore_signal(
            barrier, inc=1, device_id={"tm": (slab + d) % SLABS}, device_id_type=MESH
        )

    repeat(1, LONS, greet)

    row = lax.broadcasted_iota(jnp.int32, (TOK, TOK), 0)
    col = lax.broadcasted_iota(jnp.int32, (TOK, TOK), 1)
    c_row = column_of(row)
    for i in range(3):
        lat = row % LAT + (i - 1)
        hit = (lat >= 0) & (lat < LAT) & (col == lat * COLS + c_row)
        shift3[i * TOK : (i + 1) * TOK, :] = jnp.where(hit, 1.0, 0.0).astype(BF16)
    hit = row == (col % LAT) * COLS + column_of(col)
    order[...] = jnp.where(hit, 1.0, 0.0).astype(BF16)
    row = lax.broadcasted_iota(jnp.int32, (3 * LAT, LAT), 0)
    col = lax.broadcasted_iota(jnp.int32, (3 * LAT, LAT), 1)
    shift_h[...] = jnp.where(col == row % LAT + row // LAT - 1, 1.0, 0.0).astype(BF16)

    l_x.wait()
    x_rows = x_v.reshape(FRAMES * TOK, D)
    for f in range(FRAMES):

        def extract(j):
            lanes = pl.ds(pl.multiple_of(j * CHUNK, CHUNK), CHUNK)
            planes = dot(shift3[TOK + 2 * LAT : 2 * TOK, :], x_rows[f * TOK : (f + 1) * TOK, lanes])
            planes = planes.astype(BF16)
            edge_out[1, f, :, lanes] = planes[:LAT]
            edge_out[0, f, :, lanes] = planes[LAT:]

        repeat(0, D // CHUNK, extract)

    pl.semaphore_wait(barrier, 2 * (LONS - 1))
    halos = []
    for side, target in ((0, (lon + 1) % LONS), (1, (lon + LONS - 1) % LONS)):
        copy = pltpu.make_async_remote_copy(
            src_ref=edge_out.at[side],
            dst_ref=edge_in.at[side],
            send_sem=halo_send.at[side],
            recv_sem=halo_recv.at[side],
            device_id={"lon": target},
            device_id_type=MESH,
        )
        copy.start()
        halos.append(copy)

    l_lg.wait()
    l_cam.wait()
    n_live = live_ref[0]
    frame = lax.broadcasted_iota(jnp.int32, (FRAMES, HEADS), 0)
    live = jnp.where(frame < n_live, 1.0, 0.0).astype(F32)
    decay = jnp.exp(lg[...] * live)
    sofar = decay[0:1]
    for f in range(FRAMES):
        if f:
            sofar = sofar * decay[f : f + 1]
        for h in range(HEADS):
            at = f * HEADS + h
            dec[at : at + 1, :] = jnp.broadcast_to(decay[f : f + 1, h : h + 1], (1, HD))
            reach[at : at + 1, :] = jnp.broadcast_to(sofar[:, h : h + 1], (1, HD))
    valid = cam[...].astype(F32) * live
    lane = lax.broadcasted_iota(jnp.int32, (1, CAMS), 1)
    for n, c in enumerate((1, 2, 0, 3)):
        camera = ((lon * COLS + c) * CAMS) // LONG
        for f in range(FRAMES):
            bit = jnp.sum(jnp.where(lane == camera, valid[f : f + 1], 0.0), axis=1, keepdims=True)
            at = f * 2 * LAT + (n % 2) * LAT
            keep[n // 2, at : at + LAT, :] = jnp.broadcast_to(bit, (LAT, HD))

    l_ck.wait()

    def taps(j):
        lanes = pl.ds(pl.multiple_of(j * CHUNK, CHUNK), CHUNK)
        k = [[0.5 * ck[i, n : n + 1, lanes] for n in range(3)] for i in range(3)]

        def one(f):
            x = x_rows[pl.ds(pl.multiple_of(f * TOK, TOK), TOK), lanes]
            s = [dot(shift3[i * TOK : (i + 1) * TOK, :], x) for i in range(3)]
            place = {1: 0, 2: 1, 0: 2, 3: 3}

            def plane(i, c):
                at = place[c] * LAT
                return s[i][at : at + LAT]

            at = pl.multiple_of(f * 2 * LAT, 2 * LAT)
            for n, c in enumerate((1, 2, 0, 3)):
                total = None
                for i in range(3):
                    for m in range(3):
                        if 0 <= c + m - 1 < COLS:
                            term = k[i][m] * plane(i, c + m - 1)
                            total = term if total is None else total + term
                rows = pl.ds(at + (n % 2) * LAT, LAT)
                if n < 2:
                    mixed[0, rows, lanes] = (total * jnp.tanh(total) + total).astype(BF16)
                else:
                    partial[rows, lanes] = total

        repeat(0, FRAMES, one)

    repeat(0, D // CHUNK, taps)

    def project(half, weights, dst, masked):
        def one(j):
            lanes = pl.ds(pl.multiple_of(j * CHUNK, CHUNK), CHUNK)
            r = dot(mixed[half], weights[:, lanes])
            if masked:
                m = keep[half]
                r = r * jnp.concatenate([m, m], axis=1)
            dst[half, :, lanes] = r.astype(BF16)

        repeat(0, HK // CHUNK, one)

    l_wk.wait()
    project(0, wk, k_v, True)
    l_wv.wait()
    project(0, wv, v_v, False)
    l_wq.wait()
    project(0, wq, q_v, False)

    for copy in halos:
        copy.wait_recv()

    def edge_taps(j):
        lanes = pl.ds(pl.multiple_of(j * CHUNK, CHUNK), CHUNK)
        k = [[0.5 * ck[i, n : n + 1, lanes] for n in (0, 2)] for i in range(3)]

        def one(f):
            at = pl.multiple_of(f * 2 * LAT, 2 * LAT)
            for side in range(2):
                s = dot(shift_h[...], edge_in[side, f, :, lanes])
                rows = pl.ds(at + side * LAT, LAT)
                total = partial[rows, lanes]
                for i in range(3):
                    total = total + k[i][side] * s[i * LAT : (i + 1) * LAT]
                mixed[1, rows, lanes] = (total * jnp.tanh(total) + total).astype(BF16)

        repeat(0, FRAMES, one)

    repeat(0, D // CHUNK, edge_taps)
    project(1, wk, k_v, True)
    project(1, wv, v_v, False)

    def scan_head(h, put):
        lanes = pl.ds(pl.multiple_of(h * HD, HD), HD)
        carried = None
        for f in range(FRAMES):
            rows = pl.ds(f * 2 * LAT, 2 * LAT)
            keys = k_v[:, rows, lanes].reshape(TOK, HD)
            values = v_v[:, rows, lanes].reshape(TOK, HD)
            term = lax.dot_general(keys, values, (((0,), (0,)), ((), ())), preferred_element_type=F32)
            if f:
                term = term + dec[pl.ds(f * HEADS + h, 1), :] * carried
            carried = term
            put(f, term)

    def scan_other(n):
        def put(f, term):
            other[f, pl.ds(pl.multiple_of(n * HD, HD), HD), :] = term.astype(BF16)

        scan_head((1 - core) * 3 + n, put)

    def scan_own(n):
        def put(f, term):
            own[f, pl.ds(pl.multiple_of(n * HD, HD), HD), :] = term

        scan_head(core * 3 + n, put)

    repeat(0, 3, scan_other)
    LAST = pl.ds(FRAMES - 1, 1)
    REST = pl.ds(0, FRAMES - 1)
    parts = (LAST, REST)

    def a_copy(n):
        return pltpu.make_async_remote_copy(
            src_ref=other.at[parts[n]],
            dst_ref=abuf.at[parts[n]],
            send_sem=a_send.at[n],
            recv_sem=a_recv.at[n],
            device_id={"lon": partner},
            device_id_type=MESH,
        )

    for n in range(2):
        a_copy(n).start()
    repeat(0, 3, scan_own)

    def b_copy(n, d):
        to = (chip + d) % CHIPS
        return pltpu.make_async_remote_copy(
            src_ref=bsend.at[parts[n], pl.ds(pl.multiple_of(to * PIECE, 16), PIECE)],
            dst_ref=bbuf.at[d - 1, parts[n]],
            send_sem=b_send.at[n, d],
            recv_sem=b_recv.at[n],
            device_id={"lon": 2 * to + core},
            device_id_type=MESH,
        )

    for n, frames in enumerate(((FRAMES - 1,), tuple(range(FRAMES - 1)))):
        a_copy(n).wait_recv()
        for f in frames:

            def add(i, f=f):
                rows = pl.ds(pl.multiple_of(i * HD, HD), HD)
                total = own[f, rows, :] + abuf[f, rows, :].astype(F32)
                own[f, rows, :] = total
                bsend[f, rows, :] = total.astype(BF16)

            repeat(0, 3, add)
        repeat(1, CHIPS, lambda d, n=n: b_copy(n, d).start())

    whole = jnp.concatenate(
        [reach[(FRAMES - 1) * HEADS :, :], jnp.zeros((2, HD), F32)], axis=0
    )
    high = whole.astype(BF16)
    low = (whole - high.astype(F32)).astype(BF16)
    tmsg[PIECE:, :] = jnp.concatenate([high.astype(F32), low.astype(F32)], axis=0).astype(BF16)

    def b_wait(n):
        held = bbuf.at[:, parts[n]]
        pltpu.make_async_copy(held, held, b_recv.at[n]).wait()

    def b_sum(f):
        total = own[f, pl.ds(mine_own, PIECE), :]
        for d in range(CHIPS - 1):
            total = total + bbuf[d, f].astype(F32)
        return total

    b_wait(0)
    last = b_sum(FRAMES - 1).astype(BF16)
    tmsg[:PIECE, :] = last
    states[FRAMES - 1, pl.ds(mine, PIECE), :] = last

    def t_copy(d):
        return pltpu.make_async_remote_copy(
            src_ref=tmsg,
            dst_ref=tbuf.at[slab],
            send_sem=t_send.at[d],
            recv_sem=t_recv.at[slab],
            device_id={"tm": slab + d},
            device_id_type=MESH,
        )

    repeat(1, SLABS - slab, lambda d: t_copy(d).start())

    b_wait(1)
    for f in range(FRAMES - 1):
        states[f, pl.ds(mine, PIECE), :] = b_sum(f).astype(BF16)

    def c_copy(d):
        held = states.at[:, pl.ds(mine, PIECE)]
        return pltpu.make_async_remote_copy(
            src_ref=held,
            dst_ref=held,
            send_sem=c_send.at[d],
            recv_sem=c_recv,
            device_id={"lon": 2 * ((chip + d) % CHIPS) + core},
            device_id_type=MESH,
        )

    repeat(1, CHIPS, lambda d: c_copy(d).start())
    project(1, wq, q_v, False)

    first_head = (chip * PIECE) // HD
    second_head = jnp.minimum(first_head + 1, 2)
    spot = lax.broadcasted_iota(jnp.int32, (PIECE, HD), 0) + chip * PIECE
    in_first = spot < (first_head + 1) * HD

    def bring(s, total):
        pltpu.make_async_copy(tbuf.at[s], tbuf.at[s], t_recv.at[s]).wait()
        pair = tbuf[s, PIECE:, :].astype(F32)
        tdec[...] = pair[:8] + pair[8:]
        a = tdec[pl.ds(core * 3 + first_head, 1), :]
        b = tdec[pl.ds(core * 3 + second_head, 1), :]
        return jnp.where(in_first, a, b) * total + tbuf[s, :PIECE, :].astype(F32)

    total = lax.fori_loop(0, slab, bring, jnp.zeros((PIECE, HD), F32))
    inc[pl.ds(mine, PIECE), :] = total.astype(BF16)

    def i_copy(d):
        held = inc.at[pl.ds(mine, PIECE)]
        return pltpu.make_async_remote_copy(
            src_ref=held,
            dst_ref=held,
            send_sem=i_send.at[d],
            recv_sem=i_recv,
            device_id={"lon": (lon + d) % LONS},
            device_id_type=MESH,
        )

    repeat(1, LONS, lambda d: i_copy(d).start())

    held = states.at[:, pl.ds(0, OWN - PIECE)]
    pltpu.make_async_copy(held, held, c_recv).wait()
    held = states.at[:, pl.ds(pl.multiple_of(core * OWN, OWN), OWN)]
    d_copy = pltpu.make_async_remote_copy(
        src_ref=held,
        dst_ref=held,
        send_sem=d_send,
        recv_sem=d_recv,
        device_id={"lon": partner},
        device_id_type=MESH,
    )
    d_copy.start()
    held = inc.at[pl.ds(0, HK - PIECE)]
    pltpu.make_async_copy(held, held, i_recv).wait()
    d_copy.wait_recv()

    l_gain.wait()

    def read(f):
        rows = pl.ds(pl.multiple_of(f * 2 * LAT, 2 * LAT), 2 * LAT)
        alive = jnp.where(f < n_live, 1.0, 0.0).astype(F32)
        heads = []
        for h in range(HEADS):
            at = pl.ds(h * HD, HD)
            state = states[f, at, :].astype(F32) + reach[pl.ds(f * HEADS + h, 1), :] * inc[
                at, :
            ].astype(F32)
            readout = dot(q_v[:, rows, at].reshape(TOK, HD), state.astype(BF16))
            inverse = lax.rsqrt(jnp.mean(readout * readout, axis=-1, keepdims=True) + 1e-05)
            scale = gain[pl.ds(h * HD, HD)].reshape(1, HD) * alive
            heads.append((readout * inverse * scale).astype(BF16))
        back = dot(order[...], jnp.concatenate(heads, axis=1))
        normed[pl.ds(pl.multiple_of(f * TOK, TOK), TOK), :] = back.astype(BF16)

    repeat(0, FRAMES, read)
    l_wo.wait()
    out_rows = out_v.reshape(FRAMES * TOK, D)

    def out_copy(j):
        lanes = pl.ds(pl.multiple_of(j * CHUNK, CHUNK), CHUNK)
        return pltpu.make_async_copy(
            out_v.at[:, :, :, lanes], out_hbm.at[:, :, :, lanes], out_sem.at[j]
        )

    def emit(j):
        lanes = pl.ds(pl.multiple_of(j * CHUNK, CHUNK), CHUNK)
        out_rows[:, lanes] = dot(normed[...], wo[:, lanes]).astype(BF16)
        out_copy(j).start()

    repeat(0, D // CHUNK, emit)

    for copy in halos:
        copy.wait_send()
    for n in range(2):
        a_copy(n).wait_send()
        repeat(1, CHIPS, lambda d, n=n: b_copy(n, d).wait_send())
    repeat(1, SLABS - slab, lambda d: t_copy(d).wait_send())
    repeat(1, CHIPS, lambda d: c_copy(d).wait_send())
    repeat(1, LONS, lambda d: i_copy(d).wait_send())
    d_copy.wait_send()
    repeat(0, D // CHUNK, lambda j: out_copy(j).wait())


def local(frames_in, conv_kernel, w_query, w_key, w_value, w_out, norm_gain, log_gate, cam_valid, live_frames):
    dma = pltpu.SemaphoreType.DMA
    anywhere = pl.BlockSpec(memory_space=pl.ANY)
    return pl.pallas_call(
        kernel,
        out_shape=jax.ShapeDtypeStruct((FRAMES, LAT, COLS, D), BF16),
        in_specs=[anywhere] * 9 + [pl.BlockSpec(memory_space=pltpu.SMEM)],
        out_specs=anywhere,
        scratch_shapes=[
            pltpu.VMEM((FRAMES, LAT, COLS, D), BF16),
            pltpu.VMEM((3, 3, D), F32),
            pltpu.VMEM((D, HK), BF16),
            pltpu.VMEM((D, HK), BF16),
            pltpu.VMEM((D, HK), BF16),
            pltpu.VMEM((HK, D), BF16),
            pltpu.VMEM((HK,), F32),
            pltpu.VMEM((FRAMES, HEADS), F32),
            pltpu.VMEM((FRAMES, CAMS), jnp.int32),
            pltpu.VMEM((3 * TOK, TOK), BF16),
            pltpu.VMEM((3 * LAT, LAT), BF16),
            pltpu.VMEM((TOK, TOK), BF16),
            pltpu.VMEM((2, FRAMES, LAT, D), BF16),
            pltpu.VMEM((2, FRAMES, LAT, D), BF16),
            pltpu.VMEM((HALF, D), F32),
            pltpu.VMEM((2, HALF, D), BF16),
            pltpu.VMEM((2, HALF, HK), BF16),
            pltpu.VMEM((2, HALF, HK), BF16),
            pltpu.VMEM((2, HALF, HK), BF16),
            pltpu.VMEM((2, HALF, HD), F32),
            pltpu.VMEM((FRAMES * HEADS, HD), F32),
            pltpu.VMEM((FRAMES * HEADS, HD), F32),
            pltpu.VMEM((FRAMES, OWN, HD), BF16),
            pltpu.VMEM((FRAMES, OWN, HD), F32),
            pltpu.VMEM((FRAMES, OWN, HD), BF16),
            pltpu.VMEM((FRAMES, OWN, HD), BF16),
            pltpu.VMEM((CHIPS - 1, FRAMES, PIECE, HD), BF16),
            pltpu.VMEM((PIECE + 16, HD), BF16),
            pltpu.VMEM((SLABS, PIECE + 16, HD), BF16),
            pltpu.VMEM((8, HD), F32),
            pltpu.VMEM((FRAMES, HK, HD), BF16),
            pltpu.VMEM((HK, HD), BF16),
            pltpu.VMEM((FRAMES * TOK, HK), BF16),
            pltpu.VMEM((FRAMES, LAT, COLS, D), BF16),
            dma((9,)),
            dma((D // CHUNK,)),
            dma((2,)),
            dma((2,)),
            dma((2,)),
            dma((2,)),
            dma((2, CHIPS)),
            dma((2,)),
            dma((SLABS,)),
            dma((SLABS,)),
            dma((CHIPS,)),
            dma,
            dma,
            dma,
            dma((LONS,)),
            dma,
        ],
        compiler_params=pltpu.CompilerParams(
            collective_id=0, has_side_effects=True, vmem_limit_bytes=56 * 1024 * 1024
        ),
    )(frames_in, conv_kernel, w_query, w_key, w_value, w_out, norm_gain, log_gate, cam_valid, live_frames)


def solution(mesh):
    in_specs = (
        P("tm", None, "lon", None),
        P(),
        P(),
        P(),
        P(),
        P(),
        P(),
        P("tm", None),
        P("tm", None),
        P("tm"),
    )
    out_specs = P("tm", None, "lon", None)
    return jax.shard_map(local, mesh=mesh, in_specs=in_specs, out_specs=out_specs, check_vma=False)
```

time: 440 us -> 57.5 us (0.13)
  the two profiles are of different devices: /device:TPU:8 before, /device:TPU:1 now
where the time goes in v1:
time: 57.5 us; the launch traced here: 57.4 us
  Pallas kernels  53.7 us (93%)
  local copies, waits for them, and re-layouts  3.09 us (5%)
  between operations  0.66 us (1%)
    pallas_call x1, Pallas kernels, local(): pl.pallas_call(kernel, out_shape=jax.ShapeDtypeStruct((FRAMES, LAT, COLS,...  53.7 us
    unnamed x1, local copies, waits for them, and re-layouts  3.09 us

profile of v1, /device:TPU:1, one launch (start us, length us, event | category | flops | bytes accessed | tf_op | source)
XLA Modules:
  0.0 57.4 jit_solution(14224442171170446893)
XLA Ops:
  0.7 53.7 %shard_map.100 = bf16[4,32,4,1536]{3,2,1,0:T(4,128)(2,1)} custom-call(bf16[4,32,4,1536]{3,2,1,0:T(4,128)(2,1)} %x_hbm.1, f32[3,3,1536]{2,1,0:T(4,128)} %ck_hbm.1, bf16[1536,768]{1,0:T(8,128)(2,1)} %wq_hbm.1, bf16[1536,768]{1,0:T(8,128)(2,1)} %wk_hbm.1, bf16[1536,768]{1,0:T(8,128)(2,1)} %wv_hbm.1, bf16[768,1536]{1,0:T(8,128)(2,1)} %wo_hbm.1, f32[768]{0:T(1024)} %gain_hbm.1, ...), custom_call_target="tpu_custom_call" | custom-call | tf_op jit(solution)/shard_map/pallas_call | solution.py:504
  54.3 3.1 %copy.13 = bf16[4,32,4,1536]{3,2,1,0:T(4,128)(2,1)} copy(bf16[4,32,4,1536]{3,2,1,0:T(4,128)(2,1)} %shard_map.100) | data formatting | bytes 3145728

commit v2 on v1

v2 whole, which is shorter than its diff:
```python
import jax
import jax.numpy as jnp
from jax import lax
from jax.experimental import pallas as pl
from jax.experimental.pallas import tpu as pltpu
from jax.sharding import PartitionSpec as P

MESH = pl.DeviceIdType.MESH
F32 = jnp.float32
BF16 = jnp.bfloat16

HEADS = 6
HD = 128
CAMS = 6
FRAMES = 4
LAT = 32
COLS = 4
D = 1536
HK = HEADS * HD
TOK = LAT * COLS
LONG = 64
CHUNK = 256
HALF = FRAMES * 2 * LAT
OWN = HK // 2
CHIPS = 8
PIECE = OWN // CHIPS
PARTS = ((0, 1), (3,), (2,))
SLABS = 16
LONS = 16


def repeat(first, last, body, unroll=1):
    def step(i, carry):
        body(i)
        return carry

    lax.fori_loop(first, last, step, 0, unroll=unroll)


def dot(a, b):
    return jnp.dot(a, b, preferred_element_type=F32)


def column_of(t):
    block = t // LAT
    return jnp.where(block == 0, 1, jnp.where(block == 1, 2, jnp.where(block == 2, 0, 3)))


def kernel(
    x_hbm,
    ck_hbm,
    wq_hbm,
    wk_hbm,
    wv_hbm,
    gain_hbm,
    lg_hbm,
    cam_hbm,
    live_hbm,
    normed,
    live_ref,
    x_v,
    ck,
    wq,
    wk,
    wv,
    gain,
    lg,
    cam,
    shift3,
    shift_h,
    order,
    edge_out,
    edge_in,
    partial,
    mixed,
    q_v,
    k_v,
    v_v,
    keep,
    dec,
    reach,
    other,
    other_sum,
    own,
    own_sum,
    abuf,
    bsend,
    bbuf,
    tbuf,
    dsend,
    tdec,
    states,
    inc,
    load_sem,
    halo_send,
    halo_recv,
    a_send,
    a_recv,
    b_send,
    b_recv,
    dec_send,
    dec_recv,
    t_send,
    t_recv,
    c_send,
    c_recv,
    d_send,
    d_recv,
    i_send,
    i_recv,
    e_send,
    e_recv,
):
    lon = lax.axis_index("lon")
    slab = lax.axis_index("tm")
    core = lon % 2
    chip = lon // 2
    partner = lon + 1 - 2 * core
    half = pl.multiple_of(core * OWN, OWN)
    mine_own = pl.multiple_of(chip * PIECE, 16)
    mine = pl.multiple_of(core * OWN + chip * PIECE, 16)

    loads = []
    for n, (src, dst) in enumerate(
        (
            (x_hbm, x_v),
            (live_hbm, live_ref),
            (ck_hbm, ck),
            (lg_hbm, lg),
            (cam_hbm, cam),
            (gain_hbm, gain),
            (wk_hbm, wk),
            (wv_hbm, wv),
            (wq_hbm, wq),
        )
    ):
        copy = pltpu.make_async_copy(src, dst, load_sem.at[n])
        copy.start()
        loads.append(copy)
    l_x, l_live, l_ck, l_lg, l_cam, l_gain, l_wk, l_wv, l_wq = loads

    barrier = pltpu.get_barrier_semaphore()

    def greet(d):
        pl.semaphore_signal(
            barrier, inc=1, device_id={"lon": (lon + d) % LONS}, device_id_type=MESH
        )
        pl.semaphore_signal(
            barrier, inc=1, device_id={"tm": (slab + d) % SLABS}, device_id_type=MESH
        )

    repeat(1, LONS, greet)

    def to_lon(src, dst, send, recv, target):
        return pltpu.make_async_remote_copy(
            src_ref=src,
            dst_ref=dst,
            send_sem=send,
            recv_sem=recv,
            device_id={"lon": target},
            device_id_type=MESH,
        )

    def wait_for(held, sem):
        pltpu.make_async_copy(held, held, sem).wait()

    row = lax.broadcasted_iota(jnp.int32, (TOK, TOK), 0)
    col = lax.broadcasted_iota(jnp.int32, (TOK, TOK), 1)
    c_row = column_of(row)
    for i in range(3):
        lat = row % LAT + (i - 1)
        hit = (lat >= 0) & (lat < LAT) & (col == lat * COLS + c_row)
        shift3[i * TOK : (i + 1) * TOK, :] = jnp.where(hit, 1.0, 0.0).astype(BF16)
    hit = row == (col % LAT) * COLS + column_of(col)
    order[...] = jnp.where(hit, 1.0, 0.0).astype(BF16)
    row = lax.broadcasted_iota(jnp.int32, (3 * LAT, LAT), 0)
    col = lax.broadcasted_iota(jnp.int32, (3 * LAT, LAT), 1)
    shift_h[...] = jnp.where(col == row % LAT + row // LAT - 1, 1.0, 0.0).astype(BF16)

    l_x.wait()
    x_rows = x_v.reshape(FRAMES * TOK, D)
    for f in range(FRAMES):

        def extract(j):
            lanes = pl.ds(pl.multiple_of(j * CHUNK, CHUNK), CHUNK)
            planes = dot(shift3[TOK + 2 * LAT : 2 * TOK, :], x_rows[f * TOK : (f + 1) * TOK, lanes])
            planes = planes.astype(BF16)
            edge_out[1, f, :, lanes] = planes[:LAT]
            edge_out[0, f, :, lanes] = planes[LAT:]

        repeat(0, D // CHUNK, extract, 3)

    def halo_copy(side, f):
        target = (lon + (1 if side == 0 else LONS - 1)) % LONS
        return to_lon(
            edge_out.at[side, f],
            edge_in.at[side, f],
            halo_send.at[side, f],
            halo_recv.at[side, f],
            target,
        )

    pl.semaphore_wait(barrier, 2 * (LONS - 1))
    for f in range(FRAMES):
        for side in range(2):
            halo_copy(side, f).start()

    l_live.wait()
    l_lg.wait()
    l_cam.wait()
    n_live = live_ref[0]
    frame = lax.broadcasted_iota(jnp.int32, (FRAMES, HEADS), 0)
    live = jnp.where(frame < n_live, 1.0, 0.0).astype(F32)
    decay = jnp.exp(lg[...] * live)
    sofar = decay[0:1]
    for f in range(FRAMES):
        if f:
            sofar = sofar * decay[f : f + 1]
        for h in range(HEADS):
            at = f * HEADS + h
            dec[at : at + 1, :] = jnp.broadcast_to(decay[f : f + 1, h : h + 1], (1, HD))
            reach[at : at + 1, :] = jnp.broadcast_to(sofar[:, h : h + 1], (1, HD))
    dsend[...] = jnp.concatenate(
        [reach[(FRAMES - 1) * HEADS :, :], jnp.zeros((8 - HEADS, HD), F32)], axis=0
    )

    def dec_copy(d):
        return pltpu.make_async_remote_copy(
            src_ref=dsend,
            dst_ref=tdec.at[slab],
            send_sem=dec_send.at[d],
            recv_sem=dec_recv.at[slab],
            device_id={"tm": slab + d},
            device_id_type=MESH,
        )

    repeat(1, SLABS - slab, lambda d: dec_copy(d).start())
    valid = cam[...].astype(F32) * live
    lane = lax.broadcasted_iota(jnp.int32, (1, CAMS), 1)
    for n, c in enumerate((1, 2, 0, 3)):
        camera = ((lon * COLS + c) * CAMS) // LONG
        for f in range(FRAMES):
            bit = jnp.sum(jnp.where(lane == camera, valid[f : f + 1], 0.0), axis=1, keepdims=True)
            at = f * 2 * LAT + (n % 2) * LAT
            keep[n // 2, at : at + LAT, :] = jnp.broadcast_to(bit, (LAT, HD))

    l_ck.wait()

    def taps(j):
        lanes = pl.ds(pl.multiple_of(j * CHUNK, CHUNK), CHUNK)
        k = [[0.5 * ck[i, n : n + 1, lanes] for n in range(3)] for i in range(3)]

        def one(f):
            x = x_rows[pl.ds(pl.multiple_of(f * TOK, TOK), TOK), lanes]
            s = [dot(shift3[i * TOK : (i + 1) * TOK, :], x) for i in range(3)]
            place = {1: 0, 2: 1, 0: 2, 3: 3}

            def plane(i, c):
                at = place[c] * LAT
                return s[i][at : at + LAT]

            at = pl.multiple_of(f * 2 * LAT, 2 * LAT)
            for n, c in enumerate((1, 2, 0, 3)):
                total = None
                for i in range(3):
                    for m in range(3):
                        if 0 <= c + m - 1 < COLS:
                            term = k[i][m] * plane(i, c + m - 1)
                            total = term if total is None else total + term
                rows = pl.ds(at + (n % 2) * LAT, LAT)
                if n < 2:
                    mixed[0, rows, lanes] = (total * jnp.tanh(total) + total).astype(BF16)
                else:
                    partial[rows, lanes] = total

        repeat(0, FRAMES, one, FRAMES)

    repeat(0, D // CHUNK, taps)

    def project(side, first, count, weights, dst, masked, unroll):
        rows = pl.ds(first, count)

        def one(j):
            lanes = pl.ds(pl.multiple_of(j * CHUNK, CHUNK), CHUNK)
            r = dot(mixed[side, rows, :], weights[:, lanes])
            if masked:
                m = keep[side, rows, :]
                r = r * jnp.concatenate([m, m], axis=1)
            dst[side, rows, lanes] = r.astype(BF16)

        repeat(0, HK // CHUNK, one, unroll)

    l_wk.wait()
    project(0, 0, HALF, wk, k_v, True, 3)
    l_wv.wait()
    project(0, 0, HALF, wv, v_v, False, 3)

    l_wq.wait()
    project(0, 0, HALF, wq, q_v, False, 3)

    def edge_taps(f):
        def one(j):
            lanes = pl.ds(pl.multiple_of(j * CHUNK, CHUNK), CHUNK)
            for side in range(2):
                s = dot(shift_h[...], edge_in[side, f, :, lanes])
                rows = pl.ds(f * 2 * LAT + side * LAT, LAT)
                total = partial[rows, lanes]
                for i in range(3):
                    tap = 0.5 * ck[i, 2 * side : 2 * side + 1, lanes]
                    total = total + tap * s[i * LAT : (i + 1) * LAT]
                mixed[1, rows, lanes] = (total * jnp.tanh(total) + total).astype(BF16)

        repeat(0, D // CHUNK, one, D // CHUNK)

    def scan_heads(frames, first, carried, put):
        def one(n):
            h = first + n
            lanes = pl.ds(pl.multiple_of(h * HD, HD), HD)
            at = pl.ds(pl.multiple_of(n * HD, HD), HD)
            total = None
            for f in frames:
                rows = pl.ds(f * 2 * LAT, 2 * LAT)
                keys = k_v[:, rows, lanes].reshape(TOK, HD)
                values = v_v[:, rows, lanes].reshape(TOK, HD)
                term = lax.dot_general(
                    keys, values, (((0,), (0,)), ((), ())), preferred_element_type=F32
                )
                if f:
                    before = carried[at, :] if total is None else total
                    term = term + dec[pl.ds(f * HEADS + h, 1), :] * before
                total = term
                put(f, at, total)
            carried[at, :] = total

        repeat(0, 3, one, 3)

    def put_other(f, at, total):
        other[f, at, :] = total.astype(BF16)

    def put_own(f, at, total):
        own[f, at, :] = total

    def frames_of(p):
        return pl.ds(PARTS[p][0], len(PARTS[p]))

    def a_copy(p):
        at = frames_of(p)
        return to_lon(other.at[at], abuf.at[at], a_send.at[p], a_recv.at[p], partner)

    def b_copy(p, d):
        to = (chip + d) % CHIPS
        rows = pl.ds(pl.multiple_of(to * PIECE, 16), PIECE)
        return to_lon(
            bsend.at[frames_of(p), rows],
            bbuf.at[d - 1, frames_of(p)],
            b_send.at[p, d],
            b_recv.at[p],
            2 * to + core,
        )

    def c_copy(p, d):
        held = states.at[frames_of(p), pl.ds(mine, PIECE)]
        to = (chip + d) % CHIPS
        return to_lon(held, held, c_send.at[p, d], c_recv.at[p], 2 * to + core)

    def d_copy(p):
        held = states.at[frames_of(p), pl.ds(half, OWN)]
        return to_lon(held, held, d_send.at[p], d_recv.at[p], partner)

    def t_copy(d):
        return pltpu.make_async_remote_copy(
            src_ref=states.at[FRAMES - 1, pl.ds(mine, PIECE)],
            dst_ref=tbuf.at[slab],
            send_sem=t_send.at[d],
            recv_sem=t_recv.at[slab],
            device_id={"tm": slab + d},
            device_id_type=MESH,
        )

    def after_a(p):
        a_copy(p).wait_recv()
        for f in PARTS[p]:
            for n in range(3):
                rows = pl.ds(n * HD, HD)
                total = own[f, rows, :] + abuf[f, rows, :].astype(F32)
                own[f, rows, :] = total
                bsend[f, rows, :] = total.astype(BF16)
        repeat(1, CHIPS, lambda d: b_copy(p, d).start())

    def after_b(p):
        wait_for(bbuf.at[:, frames_of(p)], b_recv.at[p])
        for f in PARTS[p]:
            total = own[f, pl.ds(mine_own, PIECE), :]
            for d in range(CHIPS - 1):
                total = total + bbuf[d, f].astype(F32)
            states[f, pl.ds(mine, PIECE), :] = total.astype(BF16)
        if PARTS[p][0] == FRAMES - 1:
            repeat(1, SLABS - slab, lambda d: t_copy(d).start())
        repeat(1, CHIPS, lambda d: c_copy(p, d).start())

    def after_c(p):
        wait_for(states.at[frames_of(p), pl.ds(0, OWN - PIECE)], c_recv.at[p])
        d_copy(p).start()

    for group in ((0, 1), (2, 3)):
        for f in group:
            for side in range(2):
                halo_copy(side, f).wait_recv()
            edge_taps(f)
        first = group[0] * 2 * LAT
        if first:
            after_a(0)
        project(1, first, 4 * LAT, wk, k_v, True, 3)
        project(1, first, 4 * LAT, wv, v_v, False, 3)
        scan_heads(group, (1 - core) * 3, other_sum, put_other)
        if first:
            a_copy(1).start()
            a_copy(2).start()
        else:
            a_copy(0).start()
        scan_heads(group, core * 3, own_sum, put_own)
    after_a(1)
    after_a(2)
    after_b(0)
    after_b(1)
    after_b(2)
    project(1, 0, HALF, wq, q_v, False, 3)
    after_c(0)

    first_head = mine_own // HD
    second_head = jnp.minimum(first_head + 1, 2)
    spot = lax.broadcasted_iota(jnp.int32, (PIECE, HD), 0) + mine_own
    in_first = spot < (first_head + 1) * HD

    def bring(s, total):
        wait_for(tdec.at[s], dec_recv.at[s])
        wait_for(tbuf.at[s], t_recv.at[s])
        a = tdec[s, pl.ds(core * 3 + first_head, 1), :]
        b = tdec[s, pl.ds(core * 3 + second_head, 1), :]
        return jnp.where(in_first, a, b) * total + tbuf[s].astype(F32)

    total = lax.fori_loop(0, slab, bring, jnp.zeros((PIECE, HD), F32))
    inc[pl.ds(mine, PIECE), :] = total.astype(BF16)

    def i_copy(d):
        held = inc.at[pl.ds(mine, PIECE)]
        return to_lon(held, held, i_send.at[d], i_recv, (lon + 2 * d) % LONS)

    repeat(1, LONS // 2, lambda d: i_copy(d).start())
    after_c(1)
    after_c(2)
    wait_for(inc.at[pl.ds(0, OWN - PIECE)], i_recv)
    held = inc.at[pl.ds(half, OWN)]
    e_copy = to_lon(held, held, e_send, e_recv, partner)
    e_copy.start()
    for p in range(3):
        d_copy(p).wait_recv()
    e_copy.wait_recv()

    l_gain.wait()

    def read(f):
        rows = pl.ds(pl.multiple_of(f * 2 * LAT, 2 * LAT), 2 * LAT)
        alive = jnp.where(f < n_live, 1.0, 0.0).astype(F32)
        heads = []
        for h in range(HEADS):
            at = pl.ds(h * HD, HD)
            state = states[f, at, :].astype(F32) + reach[pl.ds(f * HEADS + h, 1), :] * inc[
                at, :
            ].astype(F32)
            readout = dot(q_v[:, rows, at].reshape(TOK, HD), state.astype(BF16))
            inverse = lax.rsqrt(jnp.mean(readout * readout, axis=-1, keepdims=True) + 1e-05)
            scale = gain[pl.ds(h * HD, HD)].reshape(1, HD) * alive
            heads.append((readout * inverse * scale).astype(BF16))
        back = dot(order[...], jnp.concatenate(heads, axis=1))
        normed[pl.ds(pl.multiple_of(f * TOK, TOK), TOK), :] = back.astype(BF16)

    repeat(0, FRAMES, read, FRAMES)

    for f in range(FRAMES):
        for side in range(2):
            halo_copy(side, f).wait_send()
    for p in range(3):
        a_copy(p).wait_send()
        repeat(1, CHIPS, lambda d, p=p: b_copy(p, d).wait_send())
        repeat(1, CHIPS, lambda d, p=p: c_copy(p, d).wait_send())
        d_copy(p).wait_send()
    repeat(1, SLABS - slab, lambda d: dec_copy(d).wait_send())
    repeat(1, SLABS - slab, lambda d: t_copy(d).wait_send())
    repeat(1, LONS // 2, lambda d: i_copy(d).wait_send())
    e_copy.wait_send()


def out_kernel(normed, wo, out_hbm, out_v, out_sem):
    out_rows = out_v.reshape(FRAMES * TOK, D)

    def out_copy(j):
        lanes = pl.ds(pl.multiple_of(j * CHUNK, CHUNK), CHUNK)
        return pltpu.make_async_copy(
            out_v.at[:, :, :, lanes], out_hbm.at[:, :, :, lanes], out_sem.at[j]
        )

    def emit(j):
        lanes = pl.ds(pl.multiple_of(j * CHUNK, CHUNK), CHUNK)
        out_rows[:, lanes] = dot(normed[...], wo[:, lanes]).astype(BF16)
        out_copy(j).start()

    repeat(0, D // CHUNK, emit, 2)
    repeat(0, D // CHUNK, lambda j: out_copy(j).wait())


def local(frames_in, conv_kernel, w_query, w_key, w_value, w_out, norm_gain, log_gate, cam_valid, live_frames):
    dma = pltpu.SemaphoreType.DMA
    anywhere = pl.BlockSpec(memory_space=pltpu.HBM)
    held = pl.BlockSpec(memory_space=pltpu.VMEM)
    normed = pl.pallas_call(
        kernel,
        out_shape=jax.ShapeDtypeStruct((FRAMES * TOK, HK), BF16),
        in_specs=[anywhere] * 9,
        out_specs=held,
        scratch_shapes=[
            pltpu.SMEM((1,), jnp.int32),
            pltpu.VMEM((FRAMES, LAT, COLS, D), BF16),
            pltpu.VMEM((3, 3, D), F32),
            pltpu.VMEM((D, HK), BF16),
            pltpu.VMEM((D, HK), BF16),
            pltpu.VMEM((D, HK), BF16),
            pltpu.VMEM((HK,), F32),
            pltpu.VMEM((FRAMES, HEADS), F32),
            pltpu.VMEM((FRAMES, CAMS), jnp.int32),
            pltpu.VMEM((3 * TOK, TOK), BF16),
            pltpu.VMEM((3 * LAT, LAT), BF16),
            pltpu.VMEM((TOK, TOK), BF16),
            pltpu.VMEM((2, FRAMES, LAT, D), BF16),
            pltpu.VMEM((2, FRAMES, LAT, D), BF16),
            pltpu.VMEM((HALF, D), F32),
            pltpu.VMEM((2, HALF, D), BF16),
            pltpu.VMEM((2, HALF, HK), BF16),
            pltpu.VMEM((2, HALF, HK), BF16),
            pltpu.VMEM((2, HALF, HK), BF16),
            pltpu.VMEM((2, HALF, HD), F32),
            pltpu.VMEM((FRAMES * HEADS, HD), F32),
            pltpu.VMEM((FRAMES * HEADS, HD), F32),
            pltpu.VMEM((FRAMES, OWN, HD), BF16),
            pltpu.VMEM((OWN, HD), F32),
            pltpu.VMEM((FRAMES, OWN, HD), F32),
            pltpu.VMEM((OWN, HD), F32),
            pltpu.VMEM((FRAMES, OWN, HD), BF16),
            pltpu.VMEM((FRAMES, OWN, HD), BF16),
            pltpu.VMEM((CHIPS - 1, FRAMES, PIECE, HD), BF16),
            pltpu.VMEM((SLABS, PIECE, HD), BF16),
            pltpu.VMEM((8, HD), F32),
            pltpu.VMEM((SLABS, 8, HD), F32),
            pltpu.VMEM((FRAMES, HK, HD), BF16),
            pltpu.VMEM((HK, HD), BF16),
            dma((9,)),
            dma((2, FRAMES)),
            dma((2, FRAMES)),
            dma((3,)),
            dma((3,)),
            dma((3, CHIPS)),
            dma((3,)),
            dma((SLABS,)),
            dma((SLABS,)),
            dma((SLABS,)),
            dma((SLABS,)),
            dma((3, CHIPS)),
            dma((3,)),
            dma((3,)),
            dma((3,)),
            dma((LONS // 2,)),
            dma,
            dma,
            dma,
        ],
        compiler_params=pltpu.CompilerParams(
            collective_id=0, has_side_effects=True, vmem_limit_bytes=58 * 1024 * 1024
        ),
    )(frames_in, conv_kernel, w_query, w_key, w_value, norm_gain, log_gate, cam_valid, live_frames)
    return pl.pallas_call(
        out_kernel,
        out_shape=jax.ShapeDtypeStruct((FRAMES, LAT, COLS, D), BF16),
        in_specs=[held, held],
        out_specs=anywhere,
        scratch_shapes=[
            pltpu.VMEM((FRAMES, LAT, COLS, D), BF16),
            dma((D // CHUNK,)),
        ],
        compiler_params=pltpu.CompilerParams(vmem_limit_bytes=16 * 1024 * 1024),
    )(normed, w_out)


def solution(mesh):
    in_specs = (
        P("tm", None, "lon", None),
        P(),
        P(),
        P(),
        P(),
        P(),
        P(),
        P("tm", None),
        P("tm", None),
        P("tm"),
    )
    out_specs = P("tm", None, "lon", None)
    return jax.shard_map(local, mesh=mesh, in_specs=in_specs, out_specs=out_specs, check_vma=False)
```

time: 57.5 us -> 50.3 us (0.87)
  Pallas kernels: 53.7 us -> 48.4 us
  local copies, waits for them, and re-layouts: 3.09 us -> 1.13 us
    pallas_call x1 -> x2, Pallas kernels: 53.7 us -> 48.4 us  [the longest x1 45.8 us: local(): pl.pallas_call(kernel, out_shape=jax.ShapeDtypeStruct((FRAMES * TOK, HK),...]
    unnamed x1 -> x4, local copies, waits for them, and re-layouts: 3.09 us -> 1.13 us
where the time goes in v2:
time: 50.3 us; the launch traced here: 50.2 us
  Pallas kernels  48.4 us (96%)
  local copies, waits for them, and re-layouts  1.13 us (2%)
  between operations  0.68 us (1%)
    pallas_call x1, Pallas kernels, local(): pl.pallas_call(kernel, out_shape=jax.ShapeDtypeStruct((FRAMES * TOK, HK),...  45.8 us
    pallas_call x1, Pallas kernels, local(): pl.pallas_call(out_kernel, out_shape=jax.ShapeDtypeStruct((FRAMES, LAT, C...  2.64 us
    unnamed x4, local copies, waits for them, and re-layouts  1.13 us

profile of v2, /device:TPU:1, one launch (start us, length us, event | category | flops | bytes accessed | tf_op | source)
XLA Modules:
  0.0 50.2 jit_solution(10025731782245379837)
XLA Ops:
  0.7 0.0 copy-start.1
  0.7 45.8 %shard_map.100.normed = bf16[512,768]{1,0:T(8,128)(2,1)} custom-call(bf16[4,32,4,1536]{3,2,1,0:T(4,128)(2,1)} %x_hbm.1, f32[3,3,1536]{2,1,0:T(4,128)} %ck_hbm.1, bf16[1536,768]{1,0:T(8,128)(2,1)} %wq_hbm.1, bf16[1536,768]{1,0:T(8,128)(2,1)} %wk_hbm.1, bf16[1536,768]{1,0:T(8,128)(2,1)} %wv_hbm.1, f32[768]{0:T(1024)} %gain_hbm.1, f32[4,6]{1,0:T(4,128)} %lg_hbm.1, ...), custom_call_target="tpu_custom_call" | custom-call | tf_op jit(solution)/shard_map/pallas_call | solution.py:516
  46.4 0.0 copy-done.1
  46.4 0.0 copy-start
  46.5 1.1 %copy-done = bf16[512,768]{1,0:T(8,128)(2,1)S(1)} copy-done((bf16[512,768]{1,0:T(8,128)(2,1)S(1)}, bf16[512,768]{1,0:T(8,128)(2,1)}, u32[]{:S(2)}) %copy-start) | copy-done | bytes 786456
  47.6 2.6 %shard_map.101 = bf16[4,32,4,1536]{3,2,1,0:T(4,128)(2,1)} custom-call(bf16[512,768]{1,0:T(8,128)(2,1)S(1)} %copy-done, bf16[768,1536]{1,0:T(8,128)(2,1)S(1)} %copy-done.1), custom_call_target="tpu_custom_call" | custom-call | tf_op jit(solution)/shard_map/pallas_call | solution.py:580
Async XLA Ops:
  0.7 45.8 %copy-start.1 = (bf16[768,1536]{1,0:T(8,128)(2,1)S(1)}, bf16[768,1536]{1,0:T(8,128)(2,1)}, u32[]{:S(2)}) copy-start(bf16[768,1536]{1,0:T(8,128)(2,1)} %wo.1) | copy-start | bytes 7077892
  46.4 1.1 %copy-start = (bf16[512,768]{1,0:T(8,128)(2,1)S(1)}, bf16[512,768]{1,0:T(8,128)(2,1)}, u32[]{:S(2)}) copy-start(bf16[512,768]{1,0:T(8,128)(2,1)} %shard_map.100.normed) | copy-start | bytes 2359300

commit v3 on v2

--- a/solution.py
+++ b/solution.py
@@ -52,17 +52,19 @@
     wq_hbm,
     wk_hbm,
     wv_hbm,
+    wo_hbm,
     gain_hbm,
     lg_hbm,
     cam_hbm,
     live_hbm,
-    normed,
+    out_hbm,
     live_ref,
     x_v,
     ck,
     wq,
     wk,
     wv,
+    wo,
     gain,
     lg,
     cam,
@@ -89,9 +91,14 @@
     tbuf,
     dsend,
     tdec,
+    weight,
     states,
     inc,
+    normed,
+    out_v,
     load_sem,
+    out_sem,
+
     halo_send,
     halo_recv,
     a_send,
@@ -123,21 +130,26 @@
     loads = []
     for n, (src, dst) in enumerate(
         (
-            (x_hbm, x_v),
+            (x_hbm.at[0], x_v.at[0]),
             (live_hbm, live_ref),
-            (ck_hbm, ck),
             (lg_hbm, lg),
             (cam_hbm, cam),
+            (x_hbm.at[1], x_v.at[1]),
+            (x_hbm.at[2], x_v.at[2]),
+            (x_hbm.at[3], x_v.at[3]),
+            (ck_hbm, ck),
             (gain_hbm, gain),
             (wk_hbm, wk),
             (wv_hbm, wv),
             (wq_hbm, wq),
+            (wo_hbm, wo),
         )
     ):
         copy = pltpu.make_async_copy(src, dst, load_sem.at[n])
         copy.start()
         loads.append(copy)
-    l_x, l_live, l_ck, l_lg, l_cam, l_gain, l_wk, l_wv, l_wq = loads
+    l_x0, l_live, l_lg, l_cam, l_x1, l_x2, l_x3, l_ck, l_gain, l_wk, l_wv, l_wq, l_wo = loads
+    l_x = (l_x0, l_x1, l_x2, l_x3)
 
     barrier = pltpu.get_barrier_semaphore()
 
@@ -176,34 +188,6 @@
     row = lax.broadcasted_iota(jnp.int32, (3 * LAT, LAT), 0)
     col = lax.broadcasted_iota(jnp.int32, (3 * LAT, LAT), 1)
     shift_h[...] = jnp.where(col == row % LAT + row // LAT - 1, 1.0, 0.0).astype(BF16)
-
-    l_x.wait()
-    x_rows = x_v.reshape(FRAMES * TOK, D)
-    for f in range(FRAMES):
-
-        def extract(j):
-            lanes = pl.ds(pl.multiple_of(j * CHUNK, CHUNK), CHUNK)
-            planes = dot(shift3[TOK + 2 * LAT : 2 * TOK, :], x_rows[f * TOK : (f + 1) * TOK, lanes])
-            planes = planes.astype(BF16)
-            edge_out[1, f, :, lanes] = planes[:LAT]
-            edge_out[0, f, :, lanes] = planes[LAT:]
-
-        repeat(0, D // CHUNK, extract, 3)
-
-    def halo_copy(side, f):
-        target = (lon + (1 if side == 0 else LONS - 1)) % LONS
-        return to_lon(
-            edge_out.at[side, f],
-            edge_in.at[side, f],
-            halo_send.at[side, f],
-            halo_recv.at[side, f],
-            target,
-        )
-
-    pl.semaphore_wait(barrier, 2 * (LONS - 1))
-    for f in range(FRAMES):
-        for side in range(2):
-            halo_copy(side, f).start()
 
     l_live.wait()
     l_lg.wait()
@@ -224,6 +208,15 @@
         [reach[(FRAMES - 1) * HEADS :, :], jnp.zeros((8 - HEADS, HD), F32)], axis=0
     )
 
+    valid = cam[...].astype(F32) * live
+    lane = lax.broadcasted_iota(jnp.int32, (1, CAMS), 1)
+    for n, c in enumerate((1, 2, 0, 3)):
+        camera = ((lon * COLS + c) * CAMS) // LONG
+        for f in range(FRAMES):
+            bit = jnp.sum(jnp.where(lane == camera, valid[f : f + 1], 0.0), axis=1, keepdims=True)
+            at = f * 2 * LAT + (n % 2) * LAT
+            keep[n // 2, at : at + LAT, :] = jnp.broadcast_to(bit, (LAT, HD))
+
     def dec_copy(d):
         return pltpu.make_async_remote_copy(
             src_ref=dsend,
@@ -234,15 +227,34 @@
             device_id_type=MESH,
         )
 
+    x_rows = x_v.reshape(FRAMES * TOK, D)
+
+    def halo_copy(side, f):
+        target = (lon + (1 if side == 0 else LONS - 1)) % LONS
+        return to_lon(
+            edge_out.at[side, f],
+            edge_in.at[side, f],
+            halo_send.at[side, f],
+            halo_recv.at[side, f],
+            target,
+        )
+
+    for f in range(FRAMES):
+        l_x[f].wait()
+
+        def extract(j, f=f):
+            lanes = pl.ds(pl.multiple_of(j * CHUNK, CHUNK), CHUNK)
+            planes = dot(shift3[TOK + 2 * LAT : 2 * TOK, :], x_rows[f * TOK : (f + 1) * TOK, lanes])
+            planes = planes.astype(BF16)
+            edge_out[1, f, :, lanes] = planes[:LAT]
+            edge_out[0, f, :, lanes] = planes[LAT:]
+
+        repeat(0, D // CHUNK, extract, 6)
+        if f == 0:
+            pl.semaphore_wait(barrier, 2 * (LONS - 1))
+        for side in range(2):
+            halo_copy(side, f).start()
     repeat(1, SLABS - slab, lambda d: dec_copy(d).start())
-    valid = cam[...].astype(F32) * live
-    lane = lax.broadcasted_iota(jnp.int32, (1, CAMS), 1)
-    for n, c in enumerate((1, 2, 0, 3)):
-        camera = ((lon * COLS + c) * CAMS) // LONG
-        for f in range(FRAMES):
-            bit = jnp.sum(jnp.where(lane == camera, valid[f : f + 1], 0.0), axis=1, keepdims=True)
-            at = f * 2 * LAT + (n % 2) * LAT
-            keep[n // 2, at : at + LAT, :] = jnp.broadcast_to(bit, (LAT, HD))
 
     l_ck.wait()
 
@@ -275,7 +287,7 @@
 
         repeat(0, FRAMES, one, FRAMES)
 
-    repeat(0, D // CHUNK, taps)
+    repeat(0, D // CHUNK, taps, 2)
 
     def project(side, first, count, weights, dst, masked, unroll):
         rows = pl.ds(first, count)
@@ -294,9 +306,6 @@
     project(0, 0, HALF, wk, k_v, True, 3)
     l_wv.wait()
     project(0, 0, HALF, wv, v_v, False, 3)
-
-    l_wq.wait()
-    project(0, 0, HALF, wq, q_v, False, 3)
 
     def edge_taps(f):
         def one(j):
@@ -394,8 +403,8 @@
             for d in range(CHIPS - 1):
                 total = total + bbuf[d, f].astype(F32)
             states[f, pl.ds(mine, PIECE), :] = total.astype(BF16)
-        if PARTS[p][0] == FRAMES - 1:
-            repeat(1, SLABS - slab, lambda d: t_copy(d).start())
+
+    def send_c(p):
         repeat(1, CHIPS, lambda d: c_copy(p, d).start())
 
     def after_c(p):
@@ -422,24 +431,46 @@
     after_a(1)
     after_a(2)
     after_b(0)
+    send_c(0)
     after_b(1)
+    for d in (4, 12, 5, 3, 11, 13, 2, 6, 10, 14, 8, 1, 7, 9, 15):
+
+        @pl.when(slab + d < SLABS)
+        def _(d=d):
+            t_copy(d).start()
+
+    send_c(1)
     after_b(2)
+    send_c(2)
+    l_wq.wait()
+    project(0, 0, HALF, wq, q_v, False, 3)
     project(1, 0, HALF, wq, q_v, False, 3)
-    after_c(0)
 
     first_head = mine_own // HD
     second_head = jnp.minimum(first_head + 1, 2)
     spot = lax.broadcasted_iota(jnp.int32, (PIECE, HD), 0) + mine_own
     in_first = spot < (first_head + 1) * HD
 
-    def bring(s, total):
-        wait_for(tdec.at[s], dec_recv.at[s])
-        wait_for(tbuf.at[s], t_recv.at[s])
-        a = tdec[s, pl.ds(core * 3 + first_head, 1), :]
-        b = tdec[s, pl.ds(core * 3 + second_head, 1), :]
-        return jnp.where(in_first, a, b) * total + tbuf[s].astype(F32)
-
-    total = lax.fori_loop(0, slab, bring, jnp.zeros((PIECE, HD), F32))
+    def blank(n):
+        weight[n] = jnp.zeros((PIECE, HD), F32)
+        tbuf[n] = jnp.zeros((PIECE, HD), BF16)
+
+    repeat(slab, SLABS, blank)
+
+    def weigh(n, total):
+        before = slab - 1 - n
+        weight[before] = total
+        wait_for(tdec.at[before], dec_recv.at[before])
+        a = tdec[before, pl.ds(core * 3 + first_head, 1), :]
+        b = tdec[before, pl.ds(core * 3 + second_head, 1), :]
+        return jnp.where(in_first, a, b) * total
+
+    lax.fori_loop(0, slab, weigh, jnp.ones((PIECE, HD), F32))
+    after_c(0)
+    repeat(0, slab, lambda n: wait_for(tbuf.at[n], t_recv.at[n]))
+    total = weight[0] * tbuf[0].astype(F32)
+    for n in range(1, SLABS - 1):
+        total = total + weight[n] * tbuf[n].astype(F32)
     inc[pl.ds(mine, PIECE), :] = total.astype(BF16)
 
     def i_copy(d):
@@ -460,7 +491,7 @@
     l_gain.wait()
 
     def read(f):
-        rows = pl.ds(pl.multiple_of(f * 2 * LAT, 2 * LAT), 2 * LAT)
+        rows = pl.ds(f * 2 * LAT, 2 * LAT)
         alive = jnp.where(f < n_live, 1.0, 0.0).astype(F32)
         heads = []
         for h in range(HEADS):
@@ -473,9 +504,26 @@
             scale = gain[pl.ds(h * HD, HD)].reshape(1, HD) * alive
             heads.append((readout * inverse * scale).astype(BF16))
         back = dot(order[...], jnp.concatenate(heads, axis=1))
-        normed[pl.ds(pl.multiple_of(f * TOK, TOK), TOK), :] = back.astype(BF16)
-
-    repeat(0, FRAMES, read, FRAMES)
+        normed[f * TOK : (f + 1) * TOK, :] = back.astype(BF16)
+
+    for f in range(FRAMES):
+        read(f)
+
+    l_wo.wait()
+    out_rows = out_v.reshape(FRAMES * TOK, D)
+
+    def out_copy(j):
+        lanes = pl.ds(pl.multiple_of(j * CHUNK, CHUNK), CHUNK)
+        return pltpu.make_async_copy(
+            out_v.at[:, :, :, lanes], out_hbm.at[:, :, :, lanes], out_sem.at[j]
+        )
+
+    def emit(j):
+        lanes = pl.ds(pl.multiple_of(j * CHUNK, CHUNK), CHUNK)
+        out_rows[:, lanes] = dot(normed[...], wo[:, lanes]).astype(BF16)
+        out_copy(j).start()
+
+    repeat(0, D // CHUNK, emit, 2)
 
     for f in range(FRAMES):
         for side in range(2):
@@ -489,35 +537,30 @@
     repeat(1, SLABS - slab, lambda d: t_copy(d).wait_send())
     repeat(1, LONS // 2, lambda d: i_copy(d).wait_send())
     e_copy.wait_send()
-
-
-def out_kernel(normed, wo, out_hbm, out_v, out_sem):
-    out_rows = out_v.reshape(FRAMES * TOK, D)
-
-    def out_copy(j):
-        lanes = pl.ds(pl.multiple_of(j * CHUNK, CHUNK), CHUNK)
-        return pltpu.make_async_copy(
-            out_v.at[:, :, :, lanes], out_hbm.at[:, :, :, lanes], out_sem.at[j]
-        )
-
-    def emit(j):
-        lanes = pl.ds(pl.multiple_of(j * CHUNK, CHUNK), CHUNK)
-        out_rows[:, lanes] = dot(normed[...], wo[:, lanes]).astype(BF16)
-        out_copy(j).start()
-
-    repeat(0, D // CHUNK, emit, 2)
     repeat(0, D // CHUNK, lambda j: out_copy(j).wait())
+
+
+def out_kernel(in_hbm, out_hbm, held, in_sem, out_sem):
+    fetches = [pltpu.make_async_copy(in_hbm.at[f], held.at[f], in_sem.at[f]) for f in range(FRAMES)]
+    stores = [pltpu.make_async_copy(held.at[f], out_hbm.at[f], out_sem.at[f]) for f in range(FRAMES)]
+    for copy in fetches:
+        copy.start()
+    for fetch, store in zip(fetches, stores):
+        fetch.wait()
+        store.start()
+    for copy in stores:
+        copy.wait()
 
 
 def local(frames_in, conv_kernel, w_query, w_key, w_value, w_out, norm_gain, log_gate, cam_valid, live_frames):
     dma = pltpu.SemaphoreType.DMA
     anywhere = pl.BlockSpec(memory_space=pltpu.HBM)
     held = pl.BlockSpec(memory_space=pltpu.VMEM)
-    normed = pl.pallas_call(
+    result = pl.pallas_call(
         kernel,
-        out_shape=jax.ShapeDtypeStruct((FRAMES * TOK, HK), BF16),
-        in_specs=[anywhere] * 9,
-        out_specs=held,
+        out_shape=jax.ShapeDtypeStruct((FRAMES, LAT, COLS, D), BF16),
+        in_specs=[anywhere] * 10,
+        out_specs=anywhere,
         scratch_shapes=[
             pltpu.SMEM((1,), jnp.int32),
             pltpu.VMEM((FRAMES, LAT, COLS, D), BF16),
@@ -525,6 +568,7 @@
             pltpu.VMEM((D, HK), BF16),
             pltpu.VMEM((D, HK), BF16),
             pltpu.VMEM((D, HK), BF16),
+            pltpu.VMEM((HK, D), BF16),
             pltpu.VMEM((HK,), F32),
             pltpu.VMEM((FRAMES, HEADS), F32),
             pltpu.VMEM((FRAMES, CAMS), jnp.int32),
@@ -551,9 +595,14 @@
             pltpu.VMEM((SLABS, PIECE, HD), BF16),
             pltpu.VMEM((8, HD), F32),
             pltpu.VMEM((SLABS, 8, HD), F32),
+            pltpu.VMEM((SLABS, PIECE, HD), F32),
             pltpu.VMEM((FRAMES, HK, HD), BF16),
             pltpu.VMEM((HK, HD), BF16),
-            dma((9,)),
+            pltpu.VMEM((FRAMES * TOK, HK), BF16),
+            pltpu.VMEM((FRAMES, LAT, COLS, D), BF16),
+            dma((13,)),
+            dma((D // CHUNK,)),
+
             dma((2, FRAMES)),
             dma((2, FRAMES)),
             dma((3,)),
@@ -574,20 +623,21 @@
             dma,
         ],
         compiler_params=pltpu.CompilerParams(
-            collective_id=0, has_side_effects=True, vmem_limit_bytes=58 * 1024 * 1024
+            collective_id=0, has_side_effects=True, vmem_limit_bytes=59392 * 1024
         ),
-    )(frames_in, conv_kernel, w_query, w_key, w_value, norm_gain, log_gate, cam_valid, live_frames)
+    )(frames_in, conv_kernel, w_query, w_key, w_value, w_out, norm_gain, log_gate, cam_valid, live_frames)
     return pl.pallas_call(
         out_kernel,
         out_shape=jax.ShapeDtypeStruct((FRAMES, LAT, COLS, D), BF16),
-        in_specs=[held, held],
+        in_specs=[anywhere],
         out_specs=anywhere,
         scratch_shapes=[
             pltpu.VMEM((FRAMES, LAT, COLS, D), BF16),
-            dma((D // CHUNK,)),
+            dma((FRAMES,)),
+            dma((FRAMES,)),
         ],
-        compiler_params=pltpu.CompilerParams(vmem_limit_bytes=16 * 1024 * 1024),
-    )(normed, w_out)
+        compiler_params=pltpu.CompilerParams(vmem_limit_bytes=60 * 1024 * 1024),
+    )(result)
 
 
 def solution(mesh):

time: 50.3 us -> 49.3 us (0.980)
  local copies, waits for them, and re-layouts: 1.13 us -> 0 us
    unnamed x4 -> x0, local copies, waits for them, and re-layouts: 1.13 us -> none
    pallas_call x1, Pallas kernels: 45.8 us -> 46.3 us  [local(): pl.pallas_call(kernel, out_shape=jax.ShapeDtypeStruct((FRAMES, LAT, COLS,...]
where the time goes in v3:
time: 49.3 us; the launch traced here: 49.2 us
  Pallas kernels  48.5 us (98%)
  between operations  0.66 us (1%)
    pallas_call x1, Pallas kernels, local(): pl.pallas_call(kernel, out_shape=jax.ShapeDtypeStruct((FRAMES, LAT, COLS,...  46.3 us
    pallas_call x1, Pallas kernels, local(): pl.pallas_call(out_kernel, out_shape=jax.ShapeDtypeStruct((FRAMES, LAT, C...  2.2 us

profile of v3, /device:TPU:1, one launch (start us, length us, event | category | flops | bytes accessed | tf_op | source)
XLA Modules:
  0.0 49.2 jit_solution(8569726782403757106)
XLA Ops:
  0.7 46.3 %shard_map.100.in_hbm = bf16[4,32,4,1536]{3,2,1,0:T(4,128)(2,1)} custom-call(bf16[4,32,4,1536]{3,2,1,0:T(4,128)(2,1)} %x_hbm.1, f32[3,3,1536]{2,1,0:T(4,128)} %ck_hbm.1, bf16[1536,768]{1,0:T(8,128)(2,1)} %wq_hbm.1, bf16[1536,768]{1,0:T(8,128)(2,1)} %wk_hbm.1, bf16[1536,768]{1,0:T(8,128)(2,1)} %wv_hbm.1, bf16[768,1536]{1,0:T(8,128)(2,1)} %wo_hbm.1, ...), custom_call_target="tpu_custom_call" | custom-call | tf_op jit(solution)/shard_map/pallas_call | solution.py:559
  47.0 2.2 %shard_map.101 = bf16[4,32,4,1536]{3,2,1,0:T(4,128)(2,1)} custom-call(bf16[4,32,4,1536]{3,2,1,0:T(4,128)(2,1)} %shard_map.100.in_hbm), custom_call_target="tpu_custom_call" | custom-call | tf_op jit(solution)/shard_map/pallas_call | solution.py:629

commit v4 on v3

--- a/solution.py
+++ b/solution.py
@@ -25,6 +25,8 @@
 CHIPS = 8
 PIECE = OWN // CHIPS
 PARTS = ((0, 1), (3,), (2,))
+EARLY = 2
+GATHERS = ((0, EARLY), (EARLY, FRAMES - EARLY + 1))
 SLABS = 16
 LONS = 16
 
@@ -88,12 +90,12 @@
     abuf,
     bsend,
     bbuf,
+    tsend,
     tbuf,
     dsend,
     tdec,
     weight,
     states,
-    inc,
     normed,
     out_v,
     load_sem,
@@ -113,10 +115,6 @@
     c_recv,
     d_send,
     d_recv,
-    i_send,
-    i_recv,
-    e_send,
-    e_recv,
 ):
     lon = lax.axis_index("lon")
     slab = lax.axis_index("tm")
@@ -368,17 +366,17 @@
         )
 
     def c_copy(p, d):
-        held = states.at[frames_of(p), pl.ds(mine, PIECE)]
+        held = states.at[pl.ds(*GATHERS[p]), pl.ds(mine, PIECE)]
         to = (chip + d) % CHIPS
         return to_lon(held, held, c_send.at[p, d], c_recv.at[p], 2 * to + core)
 
     def d_copy(p):
-        held = states.at[frames_of(p), pl.ds(half, OWN)]
+        held = states.at[pl.ds(*GATHERS[p]), pl.ds(half, OWN)]
         return to_lon(held, held, d_send.at[p], d_recv.at[p], partner)
 
     def t_copy(d):
         return pltpu.make_async_remote_copy(
-            src_ref=states.at[FRAMES - 1, pl.ds(mine, PIECE)],
+            src_ref=tsend,
             dst_ref=tbuf.at[slab],
             send_sem=t_send.at[d],
             recv_sem=t_recv.at[slab],
@@ -402,13 +400,18 @@
             total = own[f, pl.ds(mine_own, PIECE), :]
             for d in range(CHIPS - 1):
                 total = total + bbuf[d, f].astype(F32)
-            states[f, pl.ds(mine, PIECE), :] = total.astype(BF16)
+            if f < EARLY:
+                states[f, pl.ds(mine, PIECE), :] = total.astype(BF16)
+            else:
+                own[f, pl.ds(mine_own, PIECE), :] = total
+            if f == FRAMES - 1:
+                tsend[...] = total.astype(BF16)
 
     def send_c(p):
         repeat(1, CHIPS, lambda d: c_copy(p, d).start())
 
     def after_c(p):
-        wait_for(states.at[frames_of(p), pl.ds(0, OWN - PIECE)], c_recv.at[p])
+        wait_for(states.at[pl.ds(*GATHERS[p]), pl.ds(0, OWN - PIECE)], c_recv.at[p])
         d_copy(p).start()
 
     for group in ((0, 1), (2, 3)):
@@ -439,9 +442,7 @@
         def _(d=d):
             t_copy(d).start()
 
-    send_c(1)
     after_b(2)
-    send_c(2)
     l_wq.wait()
     project(0, 0, HALF, wq, q_v, False, 3)
     project(1, 0, HALF, wq, q_v, False, 3)
@@ -471,22 +472,17 @@
     total = weight[0] * tbuf[0].astype(F32)
     for n in range(1, SLABS - 1):
         total = total + weight[n] * tbuf[n].astype(F32)
-    inc[pl.ds(mine, PIECE), :] = total.astype(BF16)
-
-    def i_copy(d):
-        held = inc.at[pl.ds(mine, PIECE)]
-        return to_lon(held, held, i_send.at[d], i_recv, (lon + 2 * d) % LONS)
-
-    repeat(1, LONS // 2, lambda d: i_copy(d).start())
+    states[FRAMES, pl.ds(mine, PIECE), :] = total.astype(BF16)
+    for f in range(EARLY, FRAMES):
+        a = reach[pl.ds(f * HEADS + core * 3 + first_head, 1), :]
+        b = reach[pl.ds(f * HEADS + core * 3 + second_head, 1), :]
+        state = own[f, pl.ds(mine_own, PIECE), :] + jnp.where(in_first, a, b) * total
+        states[f, pl.ds(mine, PIECE), :] = state.astype(BF16)
+
+    send_c(1)
     after_c(1)
-    after_c(2)
-    wait_for(inc.at[pl.ds(0, OWN - PIECE)], i_recv)
-    held = inc.at[pl.ds(half, OWN)]
-    e_copy = to_lon(held, held, e_send, e_recv, partner)
-    e_copy.start()
-    for p in range(3):
+    for p in range(2):
         d_copy(p).wait_recv()
-    e_copy.wait_recv()
 
     l_gain.wait()
 
@@ -496,10 +492,11 @@
         heads = []
         for h in range(HEADS):
             at = pl.ds(h * HD, HD)
-            state = states[f, at, :].astype(F32) + reach[pl.ds(f * HEADS + h, 1), :] * inc[
-                at, :
-            ].astype(F32)
-            readout = dot(q_v[:, rows, at].reshape(TOK, HD), state.astype(BF16))
+            state = states[f, at, :]
+            if f < EARLY:
+                brought = reach[f * HEADS + h : f * HEADS + h + 1, :] * states[FRAMES, at, :].astype(F32)
+                state = (state.astype(F32) + brought).astype(BF16)
+            readout = dot(q_v[:, rows, at].reshape(TOK, HD), state)
             inverse = lax.rsqrt(jnp.mean(readout * readout, axis=-1, keepdims=True) + 1e-05)
             scale = gain[pl.ds(h * HD, HD)].reshape(1, HD) * alive
             heads.append((readout * inverse * scale).astype(BF16))
@@ -531,12 +528,11 @@
     for p in range(3):
         a_copy(p).wait_send()
         repeat(1, CHIPS, lambda d, p=p: b_copy(p, d).wait_send())
+    for p in range(2):
         repeat(1, CHIPS, lambda d, p=p: c_copy(p, d).wait_send())
         d_copy(p).wait_send()
     repeat(1, SLABS - slab, lambda d: dec_copy(d).wait_send())
     repeat(1, SLABS - slab, lambda d: t_copy(d).wait_send())
-    repeat(1, LONS // 2, lambda d: i_copy(d).wait_send())
-    e_copy.wait_send()
     repeat(0, D // CHUNK, lambda j: out_copy(j).wait())
 
 
@@ -592,12 +588,12 @@
             pltpu.VMEM((FRAMES, OWN, HD), BF16),
             pltpu.VMEM((FRAMES, OWN, HD), BF16),
             pltpu.VMEM((CHIPS - 1, FRAMES, PIECE, HD), BF16),
+            pltpu.VMEM((PIECE, HD), BF16),
             pltpu.VMEM((SLABS, PIECE, HD), BF16),
             pltpu.VMEM((8, HD), F32),
             pltpu.VMEM((SLABS, 8, HD), F32),
             pltpu.VMEM((SLABS, PIECE, HD), F32),
-            pltpu.VMEM((FRAMES, HK, HD), BF16),
-            pltpu.VMEM((HK, HD), BF16),
+            pltpu.VMEM((FRAMES + 1, HK, HD), BF16),
             pltpu.VMEM((FRAMES * TOK, HK), BF16),
             pltpu.VMEM((FRAMES, LAT, COLS, D), BF16),
             dma((13,)),
@@ -617,10 +613,6 @@
             dma((3,)),
             dma((3,)),
             dma((3,)),
-            dma((LONS // 2,)),
-            dma,
-            dma,
-            dma,
         ],
         compiler_params=pltpu.CompilerParams(
             collective_id=0, has_side_effects=True, vmem_limit_bytes=59392 * 1024

time: 49.3 us -> 47.1 us (0.955)
  Pallas kernels: 48.5 us -> 46.4 us
    pallas_call x1, Pallas kernels: 46.3 us -> 44.2 us  [local(): pl.pallas_call(kernel, out_shape=jax.ShapeDtypeStruct((FRAMES, LAT, COLS,...]
where the time goes in v4:
time: 47.1 us; the launch traced here: 47 us
  Pallas kernels  46.4 us (99%)
  between operations  0.66 us (1%)
    pallas_call x1, Pallas kernels, local(): pl.pallas_call(kernel, out_shape=jax.ShapeDtypeStruct((FRAMES, LAT, COLS,...  44.2 us
    pallas_call x1, Pallas kernels, local(): pl.pallas_call(out_kernel, out_shape=jax.ShapeDtypeStruct((FRAMES, LAT, C...  2.2 us

profile of v4, /device:TPU:1, one launch (start us, length us, event | category | flops | bytes accessed | tf_op | source)
XLA Modules:
  0.0 47.0 jit_solution(169308456540996226)
XLA Ops:
  0.7 44.2 %shard_map.100.in_hbm = bf16[4,32,4,1536]{3,2,1,0:T(4,128)(2,1)} custom-call(bf16[4,32,4,1536]{3,2,1,0:T(4,128)(2,1)} %x_hbm.1, f32[3,3,1536]{2,1,0:T(4,128)} %ck_hbm.1, bf16[1536,768]{1,0:T(8,128)(2,1)} %wq_hbm.1, bf16[1536,768]{1,0:T(8,128)(2,1)} %wk_hbm.1, bf16[1536,768]{1,0:T(8,128)(2,1)} %wv_hbm.1, bf16[768,1536]{1,0:T(8,128)(2,1)} %wo_hbm.1, ...), custom_call_target="tpu_custom_call" | custom-call | tf_op jit(solution)/shard_map/pallas_call | solution.py:555
  44.8 2.2 %shard_map.101 = bf16[4,32,4,1536]{3,2,1,0:T(4,128)(2,1)} custom-call(bf16[4,32,4,1536]{3,2,1,0:T(4,128)(2,1)} %shard_map.100.in_hbm), custom_call_target="tpu_custom_call" | custom-call | tf_op jit(solution)/shard_map/pallas_call | solution.py:621

commit v5 on v4

--- a/solution.py
+++ b/solution.py
@@ -23,6 +23,7 @@
 HALF = FRAMES * 2 * LAT
 OWN = HK // 2
 CHIPS = 8
+XS = 4
 PIECE = OWN // CHIPS
 PARTS = ((0, 1), (3,), (2,))
 EARLY = 2
@@ -113,6 +114,7 @@
     t_recv,
     c_send,
     c_recv,
+    across_recv,
     d_send,
     d_recv,
 ):
@@ -410,8 +412,30 @@
     def send_c(p):
         repeat(1, CHIPS, lambda d: c_copy(p, d).start())
 
+    def row_copy(at, k, sem):
+        held = states.at[pl.ds(*GATHERS[0]), pl.ds(at, PIECE)]
+        to = (chip // XS) * XS + (chip + k) % XS
+        return to_lon(held, held, c_send.at[0, sem], c_recv.at[0], 2 * to + core)
+
+    def across_copy():
+        held = states.at[pl.ds(*GATHERS[0]), pl.ds(mine, PIECE)]
+        to = (chip + XS) % CHIPS
+        return to_lon(held, held, c_send.at[0, XS], across_recv, 2 * to + core)
+
+    def send_early():
+        across_copy().start()
+        for k in range(1, XS):
+            row_copy(mine, k, k).start()
+
+    def pass_early():
+        across_copy().wait_recv()
+        at = pl.multiple_of(core * OWN + (chip + XS) % CHIPS * PIECE, 16)
+        for k in range(1, XS):
+            row_copy(at, k, XS + k).start()
+
     def after_c(p):
-        wait_for(states.at[pl.ds(*GATHERS[p]), pl.ds(0, OWN - PIECE)], c_recv.at[p])
+        pieces = OWN - PIECE if p else OWN - 2 * PIECE
+        wait_for(states.at[pl.ds(*GATHERS[p]), pl.ds(0, pieces)], c_recv.at[p])
         d_copy(p).start()
 
     for group in ((0, 1), (2, 3)):
@@ -434,7 +458,7 @@
     after_a(1)
     after_a(2)
     after_b(0)
-    send_c(0)
+    send_early()
     after_b(1)
     for d in (4, 12, 5, 3, 11, 13, 2, 6, 10, 14, 8, 1, 7, 9, 15):
 
@@ -467,7 +491,7 @@
         return jnp.where(in_first, a, b) * total
 
     lax.fori_loop(0, slab, weigh, jnp.ones((PIECE, HD), F32))
-    after_c(0)
+    pass_early()
     repeat(0, slab, lambda n: wait_for(tbuf.at[n], t_recv.at[n]))
     total = weight[0] * tbuf[0].astype(F32)
     for n in range(1, SLABS - 1):
@@ -480,6 +504,7 @@
         states[f, pl.ds(mine, PIECE), :] = state.astype(BF16)
 
     send_c(1)
+    after_c(0)
     after_c(1)
     for p in range(2):
         d_copy(p).wait_recv()
@@ -611,6 +636,7 @@
             dma((SLABS,)),
             dma((3, CHIPS)),
             dma((3,)),
+            dma,
             dma((3,)),
             dma((3,)),
         ],

time: 47.1 us -> 46.9 us (level)
  no operation moved by 1% of the time
where the time goes in v5:
time: 46.9 us; the launch traced here: 46.8 us
  Pallas kernels  46.2 us (99%)
  between operations  0.66 us (1%)
    pallas_call x1, Pallas kernels, local(): pl.pallas_call(kernel, out_shape=jax.ShapeDtypeStruct((FRAMES, LAT, COLS,...  44 us
    pallas_call x1, Pallas kernels, local(): pl.pallas_call(out_kernel, out_shape=jax.ShapeDtypeStruct((FRAMES, LAT, C...  2.2 us

profile of v5, /device:TPU:1, one launch (start us, length us, event | category | flops | bytes accessed | tf_op | source)
XLA Modules:
  0.0 46.8 jit_solution(466750064999702639)
XLA Ops:
  0.7 44.0 %shard_map.100.in_hbm = bf16[4,32,4,1536]{3,2,1,0:T(4,128)(2,1)} custom-call(bf16[4,32,4,1536]{3,2,1,0:T(4,128)(2,1)} %x_hbm.1, f32[3,3,1536]{2,1,0:T(4,128)} %ck_hbm.1, bf16[1536,768]{1,0:T(8,128)(2,1)} %wq_hbm.1, bf16[1536,768]{1,0:T(8,128)(2,1)} %wk_hbm.1, bf16[1536,768]{1,0:T(8,128)(2,1)} %wv_hbm.1, bf16[768,1536]{1,0:T(8,128)(2,1)} %wo_hbm.1, ...), custom_call_target="tpu_custom_call" | custom-call | tf_op jit(solution)/shard_map/pallas_call | solution.py:580
  44.6 2.2 %shard_map.101 = bf16[4,32,4,1536]{3,2,1,0:T(4,128)(2,1)} custom-call(bf16[4,32,4,1536]{3,2,1,0:T(4,128)(2,1)} %shard_map.100.in_hbm), custom_call_target="tpu_custom_call" | custom-call | tf_op jit(solution)/shard_map/pallas_call | solution.py:647

commit v6 on v5

--- a/solution.py
+++ b/solution.py
@@ -506,30 +506,35 @@
     send_c(1)
     after_c(0)
     after_c(1)
+
+    l_gain.wait()
+
+    for h in range(HEADS):
+        dec[h : h + 1, :] = gain[pl.ds(h * HD, HD)].reshape(1, HD)
+
+    def read_heads(first):
+        for f in range(FRAMES):
+            rows = pl.ds(f * 2 * LAT, 2 * LAT)
+            alive = jnp.where(f < n_live, 1.0, 0.0).astype(F32)
+            for n in range(3):
+                h = first + n
+                at = pl.ds(pl.multiple_of(h * HD, HD), HD)
+                state = states[f, at, :]
+                if f < EARLY:
+                    brought = reach[pl.ds(f * HEADS + h, 1), :] * states[FRAMES, at, :].astype(F32)
+                    state = (state.astype(F32) + brought).astype(BF16)
+                readout = dot(q_v[:, rows, at].reshape(TOK, HD), state)
+                inverse = lax.rsqrt(jnp.mean(readout * readout, axis=-1, keepdims=True) + 1e-05)
+                scale = dec[pl.ds(h, 1), :] * alive
+                k_v[:, rows, at] = (readout * inverse * scale).astype(BF16).reshape(2, 2 * LAT, HD)
+
+    read_heads(core * 3)
     for p in range(2):
         d_copy(p).wait_recv()
-
-    l_gain.wait()
-
-    def read(f):
-        rows = pl.ds(f * 2 * LAT, 2 * LAT)
-        alive = jnp.where(f < n_live, 1.0, 0.0).astype(F32)
-        heads = []
-        for h in range(HEADS):
-            at = pl.ds(h * HD, HD)
-            state = states[f, at, :]
-            if f < EARLY:
-                brought = reach[f * HEADS + h : f * HEADS + h + 1, :] * states[FRAMES, at, :].astype(F32)
-                state = (state.astype(F32) + brought).astype(BF16)
-            readout = dot(q_v[:, rows, at].reshape(TOK, HD), state)
-            inverse = lax.rsqrt(jnp.mean(readout * readout, axis=-1, keepdims=True) + 1e-05)
-            scale = gain[pl.ds(h * HD, HD)].reshape(1, HD) * alive
-            heads.append((readout * inverse * scale).astype(BF16))
-        back = dot(order[...], jnp.concatenate(heads, axis=1))
-        normed[f * TOK : (f + 1) * TOK, :] = back.astype(BF16)
-
+    read_heads((1 - core) * 3)
     for f in range(FRAMES):
-        read(f)
+        heads = k_v[:, pl.ds(f * 2 * LAT, 2 * LAT), :].reshape(TOK, HK)
+        normed[f * TOK : (f + 1) * TOK, :] = dot(order[...], heads).astype(BF16)
 
     l_wo.wait()
     out_rows = out_v.reshape(FRAMES * TOK, D)

time: 46.9 us -> 46.2 us (0.985)
  Pallas kernels: 46.2 us -> 45.5 us
    pallas_call x1, Pallas kernels: 44 us -> 43.3 us  [local(): pl.pallas_call(kernel, out_shape=jax.ShapeDtypeStruct((FRAMES, LAT, COLS,...]
where the time goes in v6:
time: 46.2 us; the launch traced here: 46.1 us
  Pallas kernels  45.5 us (98%)
  between operations  0.66 us (1%)
    pallas_call x1, Pallas kernels, local(): pl.pallas_call(kernel, out_shape=jax.ShapeDtypeStruct((FRAMES, LAT, COLS,...  43.3 us
    pallas_call x1, Pallas kernels, local(): pl.pallas_call(out_kernel, out_shape=jax.ShapeDtypeStruct((FRAMES, LAT, C...  2.2 us

profile of v6, /device:TPU:1, one launch (start us, length us, event | category | flops | bytes accessed | tf_op | source)
XLA Modules:
  0.0 46.1 jit_solution(15855251272069105604)
XLA Ops:
  0.7 43.3 %shard_map.100.in_hbm = bf16[4,32,4,1536]{3,2,1,0:T(4,128)(2,1)} custom-call(bf16[4,32,4,1536]{3,2,1,0:T(4,128)(2,1)} %x_hbm.1, f32[3,3,1536]{2,1,0:T(4,128)} %ck_hbm.1, bf16[1536,768]{1,0:T(8,128)(2,1)} %wq_hbm.1, bf16[1536,768]{1,0:T(8,128)(2,1)} %wk_hbm.1, bf16[1536,768]{1,0:T(8,128)(2,1)} %wv_hbm.1, bf16[768,1536]{1,0:T(8,128)(2,1)} %wo_hbm.1, ...), custom_call_target="tpu_custom_call" | custom-call | tf_op jit(solution)/shard_map/pallas_call | solution.py:585
  43.9 2.2 %shard_map.101 = bf16[4,32,4,1536]{3,2,1,0:T(4,128)(2,1)} custom-call(bf16[4,32,4,1536]{3,2,1,0:T(4,128)(2,1)} %shard_map.100.in_hbm), custom_call_target="tpu_custom_call" | custom-call | tf_op jit(solution)/shard_map/pallas_call | solution.py:652
